TPU v7x, 128 devices: a whole 4x4x4 slice. The times are simulated.
128 devices in a mesh: dp: 16 (over y_lo, z, core), seq: 8 (over x, y_hi).
Axes of the slice: x: 4, y: 4 (y_hi: 2, y_lo: 2; y = y_hi * 2 + y_lo), z: 4, core: 2. Of those that a mesh axis runs over, the one named last changes fastest.
Arguments:
- query: bfloat16 [16, 3072, 1536], P('dp', 'seq'), may hold values from -8 to 8
- key_states: bfloat16 [16, 3072, 1536], P('dp', 'seq'), may hold values from -8 to 8
- value_states: bfloat16 [16, 3072, 1536], P('dp', 'seq'), may hold values from -6 to 6
- grad_out: bfloat16 [16, 3072, 3072], P('dp', 'seq'), may hold values from -6 to 6
- w_out: bfloat16 [1536, 3072], P('dp'), may hold values from -0.15625 to 0.15625
- block_index: int32 [24, 24, 8], replicated, may hold values from 0 to 23, as said below
- block_count: int32 [24, 24], replicated, may hold values from 1 to 8, as said below
Outputs:
- grad_query: bfloat16 [16, 3072, 1536], P('dp', 'seq')
- grad_key: bfloat16 [16, 3072, 1536], P('dp', 'seq')
- grad_value: bfloat16 [16, 3072, 1536], P('dp', 'seq')
- grad_weight: float32 [1536, 3072], P(('seq', 'dp'))
Inputs may be any that keep to these rules, and one draw needn't show every extreme that they name: `block_index`: entry 0 of row [h, i] is i; the 8 entries of a row are distinct blocks within circular distance 8 // 2 of i. `block_count`: every head has a query block with count 8.
All inputs are finite; a program needn't handle non-finite values.
Results may differ from a plain program's by a relative error of at most 0.022.
Values may be sent and summed in bfloat16 or wider, within the bound.
A program may use at most 128 MiB of HBM per device.

v0:
```python
import jax
import jax.numpy as jnp
from jax import lax
from jax.sharding import PartitionSpec as P

HDIM = 64


def block_attention(query_f, key_f, value_f, index, count):

    def one_head(q_head, k_head, v_head, ids_head, cnt_head):
        blocks = ids_head.shape[0]
        slots = ids_head.shape[1]
        width = q_head.shape[0] // blocks
        hdim = q_head.shape[1]
        scale_factor = hdim ** (-0.5)
        key_blocks = k_head.reshape(blocks, width, hdim)
        value_blocks = v_head.reshape(blocks, width, hdim)
        query_blocks = q_head.reshape(blocks, width, hdim)

        @jax.checkpoint
        def one_block(items):
            q_rows, ids, cnt = items
            keys = key_blocks[ids].reshape(slots * width, hdim).astype(jnp.bfloat16)
            values = value_blocks[ids].reshape(slots * width, hdim).astype(jnp.bfloat16)
            scores = (
                lax.dot_general(
                    q_rows.astype(jnp.bfloat16),
                    keys,
                    (((1,), (1,)), ((), ())),
                    preferred_element_type=jnp.float32,
                )
                * scale_factor
            )
            live = jnp.broadcast_to((jnp.arange(slots) < cnt)[:, None], (slots, width)).reshape(-1)
            scores = jnp.where(live[None, :], scores, jnp.float32(-1e30))
            top = jnp.max(scores, axis=1, keepdims=True)
            weights = jnp.exp(scores - top)
            probs = weights / jnp.sum(weights, axis=1, keepdims=True)
            return jnp.dot(probs.astype(jnp.bfloat16), values, preferred_element_type=jnp.float32)

        result = lax.map(one_block, (query_blocks, ids_head, cnt_head))
        return result.reshape(blocks * width, hdim)

    return jax.vmap(one_head, in_axes=(1, 1, 1, 0, 0), out_axes=1)(
        query_f, key_f, value_f, index, count
    )


def video_backward(query_v, key_v, value_v, d_attn, index, count):
    seqlen, hd_all = query_v.shape
    heads = index.shape[0]
    hdim = hd_all // heads

    def shape_heads(array):
        return array.astype(jnp.float32).reshape(seqlen, heads, hdim)

    def attend(q_arr, k_arr, v_arr):
        return block_attention(q_arr, k_arr, v_arr, index, count)

    def flatten(array):
        return array.reshape(seqlen, hd_all).astype(jnp.bfloat16)

    attn, pull = jax.vjp(attend, shape_heads(query_v), shape_heads(key_v), shape_heads(value_v))
    grad_q, grad_k, grad_v = pull(shape_heads(d_attn))
    return (flatten(attn), flatten(grad_q), flatten(grad_k), flatten(grad_v))


def output_gradient(dy_rows, w_out):
    return lax.dot_general(
        dy_rows,
        lax.all_gather(w_out, "dp", axis=0, tiled=True),
        (((1,), (1,)), ((), ())),
        preferred_element_type=jnp.float32,
    ).astype(jnp.bfloat16)[None]


def swap_groups(columns, outer, inner):
    rows = columns.shape[0]
    piece_cols = columns.shape[1] // (outer * inner)
    return (
        columns.reshape(rows, outer, inner, piece_cols)
        .transpose(0, 2, 1, 3)
        .reshape(rows, columns.shape[1])
    )


def make_term(columns, dy_rows):
    return lax.dot_general(
        columns, dy_rows, (((0,), (0,)), ((), ())), preferred_element_type=jnp.float32
    )


def local(query, key_states, value_states, grad_out, w_out, block_index, block_count):
    tok_rows = query.shape[1]
    hd_all = query.shape[2]
    n_seq = lax.axis_size("seq")
    n_dp = lax.axis_size("dp")
    per_dev = hd_all // HDIM // n_seq
    dy_rows = grad_out[0]
    d_attn = output_gradient(dy_rows, w_out)
    q_heads, k_heads, v_heads, d_heads = (
        lax.all_to_all(query, "seq", split_axis=2, concat_axis=1, tiled=True),
        lax.all_to_all(key_states, "seq", split_axis=2, concat_axis=1, tiled=True),
        lax.all_to_all(value_states, "seq", split_axis=2, concat_axis=1, tiled=True),
        lax.all_to_all(d_attn, "seq", split_axis=2, concat_axis=1, tiled=True),
    )
    first_head = lax.axis_index("seq") * per_dev
    index_mine = lax.dynamic_slice_in_dim(block_index, first_head, per_dev, 0)
    count_mine = lax.dynamic_slice_in_dim(block_count, first_head, per_dev, 0)
    attn_b, grad_q, grad_k, grad_v = video_backward(
        q_heads[0], k_heads[0], v_heads[0], d_heads[0], index_mine, count_mine
    )
    scale_value = float(tok_rows * n_seq * n_dp) ** (-0.5)
    back = (
        lax.all_to_all(grad_q[None], "seq", split_axis=1, concat_axis=2, tiled=True),
        lax.all_to_all(grad_k[None], "seq", split_axis=1, concat_axis=2, tiled=True),
        lax.all_to_all(grad_v[None], "seq", split_axis=1, concat_axis=2, tiled=True),
        lax.all_to_all(attn_b[None], "seq", split_axis=1, concat_axis=2, tiled=True),
    )
    reordered = swap_groups(back[3][0], n_seq, n_dp)
    summed = lax.psum_scatter(
        make_term(reordered, dy_rows), ("dp", "seq"), scatter_dimension=0, tiled=True
    )
    return (back[0], back[1], back[2], summed * scale_value)


def solution(mesh):
    return jax.shard_map(
        local,
        mesh=mesh,
        in_specs=(
            P("dp", "seq", None),
            P("dp", "seq", None),
            P("dp", "seq", None),
            P("dp", "seq", None),
            P("dp", None),
            P(),
            P(),
        ),
        out_specs=(
            P("dp", "seq", None),
            P("dp", "seq", None),
            P("dp", "seq", None),
            P(("seq", "dp"), None),
        ),
        check_vma=False,
    )
```

profile of v0, /device:TPU:116, one launch (start us, length us, event | category | flops | bytes accessed | tf_op | source)
XLA Modules:
  0.0 2397.6 jit_solution(12633262035138286907)
XLA Ops:
  14.6 10.1 reduce.2
  39.7 11.1 reduce.4
  66.9 11.1 reduce.5
  130.5 293.6 %while.31 = (s32[]{:T(128)}, bf16[24,3,128,64]{2,3,1,0:T(8,128)(2,1)}, s32[24,3]{1,0:T(8,128)S(1)}, bf16[24,3,128,64]{2,3,1,0:T(8,128)(2,1)}, s32[24,3,8]{2,0,1:...) while((s32[]{:T(128)}, ...), condition=%wide.region_12.13_spmd.clone, body=%wide.region_9.12_spmd.clone.sunk | while | flops 103023832 | bytes 6062017 | solution.py:42
  431.9 19.3 reduce.9
  455.7 7.6 all-to-all-start.7
  463.4 7.6 fusion.57
  477.6 11.1 reduce.3
  539.0 867.7 %while.30 = (s32[]{:T(128)}, f32[3,24,128,64]{2,3,1,0:T(8,128)}, f32[3,24,128,64]{2,3,1,0:T(8,128)}, bf16[24,3,128,64]{2,3,1,0:T(8,128)(2,1)}, bf16[24,3,128,64]...) while((s32[]{:T(128)}, f32[3,24,128,64]{2,3,1,0:T(8,128)}, ...), condition=%wide.region_8.9_spmd, body=%wide.region_0.8_spmd.sunk | while | flops 268419392 | bytes 53835932 | solution.py:42
  1414.6 19.5 reduce.6
  1446.0 9.1 fusion.58
  1457.0 7.5 copy.90
  1464.5 19.3 reduce.7
  1488.4 7.5 all-to-all-start.5
  1495.9 549.9 %fusion.2 = f32[16,3072]{1,0:T(8,128)} fusion(f32[1536,3072]{1,0:T(8,128)} %fusion.58), kind=kCustom, calls=%all-reduce-scatter | all-reduce-scatter fusion | flops 6291457 | bytes 19070976
  2063.2 14.4 collective-permute-start.26
  2091.3 11.6 collective-permute-start.20
  2104.9 18.2 collective-permute-start.18
  2134.0 7.5 copy.94
  2141.5 19.3 reduce.8
  2187.4 14.0 collective-permute-done.14
  2207.6 9.2 collective-permute-start.6
  2237.0 10.8 collective-permute-start.1
  2257.0 84.8 %concatenate.20 = f32[524,3072]{1,0:T(8,128)} concatenate(f32[12,3072]{1,0:T(8,128)S(1)} %copy-done.12, f32[16,3072]{1,0:T(8,128)} %collective-permute-done.30, f32[16,3072]{1,0:T(8,128)} %collective-permute-done.29, f32[16,3072]{1,0:T(8,128)} %collective-permute-done.28, f32[16,3072]{1,0:T(8,128)} %collective-permute-done.27, f32[16,3072]{1,0:T(8,128)} %collective-permute-done.26, ...), dimensions={0} | concatenate | bytes 12877824
  (1399 shorter events, 1497.6 us)
Async XLA Ops:
  80.2 34.7 %all-to-all-start.3 = ((bf16[8,2,36864]{2,1,0:T(2,128)(2,1)}), bf16[8,2,36864]{2,1,0:T(2,128)(2,1)}, u32[]{:S(2)}, u32[]{:S(2)}) async-start(bf16[8,2,36864]{2,1,0:T(2,128)(2,1)} %reshape.370), calls=%async_computation.3 | async-start | bytes 2359296 | tf_op jit(solution)/shard_map/all_to_all | solution.py:105
  87.5 376.0 %all-gather.2.cloned.1.call-start = ((), (), s32[]{:S(2)}) async-start(), calls=%async_computation.8 | async-start | bytes 10027008 | tf_op jit(solution)/shard_map/all_gather | solution.py:72
  455.7 35.2 %all-to-all-start.7 = ((bf16[8,2,36864]{2,1,0:T(2,128)(2,1)}), bf16[8,2,36864]{2,1,0:T(2,128)(2,1)S(1)}, u32[]{:S(2)}, u32[]{:S(2)}) async-start(bf16[8,2,36864]{2,1,0:T(2,128)(2,1)} %reshape.378), calls=%async_computation.7 | async-start | bytes 2359296 | tf_op jit(solution)/shard_map/all_to_all | solution.py:119
  1438.6 49.7 %all-to-all-start.4 = ((bf16[8,2,36864]{2,1,0:T(2,128)(2,1)}), bf16[8,2,36864]{2,1,0:T(2,128)(2,1)}, u32[]{:S(2)}, u32[]{:S(2)}) async-start(bf16[8,2,36864]{2,1,0:T(2,128)(2,1)} %reshape.372), calls=%async_computation.4 | async-start | bytes 2359296 | tf_op jit(solution)/shard_map/all_to_all | solution.py:116
  1488.4 677.0 %all-to-all-start.5 = ((bf16[8,2,36864]{2,1,0:T(2,128)(2,1)}), bf16[8,2,36864]{2,1,0:T(2,128)(2,1)}, u32[]{:S(2)}, u32[]{:S(2)}) async-start(bf16[8,2,36864]{2,1,0:T(2,128)(2,1)} %reshape.374), calls=%async_computation.5 | async-start | bytes 2359296 | tf_op jit(solution)/shard_map/all_to_all | solution.py:117
  2045.8 31.9 %collective-permute-start.30 = (f32[16,3072]{1,0:T(8,128)}, f32[16,3072]{1,0:T(8,128)}, u32[]{:S(2)}, u32[]{:S(2)}) collective-permute-start(f32[16,3072]{1,0:T(8,128)} %fusion.2), channel_id=1, source_target_pairs={{0,31},{1,32},{2,33},{3,34},{4,35},{5,36},{6,37},{7,38},{8,39},{9,... | collective-permute-start | bytes 589832
  2060.1 27.2 %collective-permute-start.27 = (f32[16,3072]{1,0:T(8,128)}, f32[16,3072]{1,0:T(8,128)}, u32[]{:S(2)}, u32[]{:S(2)}) collective-permute-start(f32[16,3072]{1,0:T(8,128)} %fusion.2), channel_id=1, source_target_pairs={{0,28},{1,29},{2,30},{3,31},{4,32},{5,33},{6,34},{7,35},{8,36},{9,... | collective-permute-start | bytes 589832
  2087.4 35.7 %collective-permute-start.22 = (f32[16,3072]{1,0:T(8,128)}, f32[16,3072]{1,0:T(8,128)}, u32[]{:S(2)}, u32[]{:S(2)}) collective-permute-start(f32[16,3072]{1,0:T(8,128)} %fusion.2), channel_id=1, source_target_pairs={{0,23},{1,24},{2,25},{3,26},{4,27},{5,28},{6,29},{7,30},{8,31},{9,... | collective-permute-start | bytes 589832
  2089.3 37.6 %collective-permute-start.21 = (f32[16,3072]{1,0:T(8,128)}, f32[16,3072]{1,0:T(8,128)}, u32[]{:S(2)}, u32[]{:S(2)}) collective-permute-start(f32[16,3072]{1,0:T(8,128)} %fusion.2), channel_id=1, source_target_pairs={{0,22},{1,23},{2,24},{3,25},{4,26},{5,27},{6,28},{7,29},{8,30},{9,... | collective-permute-start | bytes 589832
  2091.3 38.6 %collective-permute-start.20 = (f32[16,3072]{1,0:T(8,128)}, f32[16,3072]{1,0:T(8,128)}, u32[]{:S(2)}, u32[]{:S(2)}) collective-permute-start(f32[16,3072]{1,0:T(8,128)} %fusion.2), channel_id=1, source_target_pairs={{0,21},{1,22},{2,23},{3,24},{4,25},{5,26},{6,27},{7,28},{8,29},{9,... | collective-permute-start | bytes 589832
  2102.9 69.8 %collective-permute-start.19 = (f32[16,3072]{1,0:T(8,128)}, f32[16,3072]{1,0:T(8,128)}, u32[]{:S(2)}, u32[]{:S(2)}) collective-permute-start(f32[16,3072]{1,0:T(8,128)} %fusion.2), channel_id=1, source_target_pairs={{0,20},{1,21},{2,22},{3,23},{4,24},{5,25},{6,26},{7,27},{8,28},{9,... | collective-permute-start | bytes 589832
  2104.9 69.8 %collective-permute-start.18 = (f32[16,3072]{1,0:T(8,128)}, f32[16,3072]{1,0:T(8,128)}, u32[]{:S(2)}, u32[]{:S(2)}) collective-permute-start(f32[16,3072]{1,0:T(8,128)} %fusion.2), channel_id=1, source_target_pairs={{0,19},{1,20},{2,21},{3,22},{4,23},{5,24},{6,25},{7,26},{8,27},{9,... | collective-permute-start | bytes 589832
  2123.1 53.7 %collective-permute-start.17 = (f32[16,3072]{1,0:T(8,128)}, f32[16,3072]{1,0:T(8,128)}, u32[]{:S(2)}, u32[]{:S(2)}) collective-permute-start(f32[16,3072]{1,0:T(8,128)} %fusion.2), channel_id=1, source_target_pairs={{0,18},{1,19},{2,20},{3,21},{4,22},{5,23},{6,24},{7,25},{8,26},{9,... | collective-permute-start | bytes 589832
  2126.9 52.5 %collective-permute-start.16 = (f32[16,3072]{1,0:T(8,128)}, f32[16,3072]{1,0:T(8,128)}, u32[]{:S(2)}, u32[]{:S(2)}) collective-permute-start(f32[16,3072]{1,0:T(8,128)} %fusion.2), channel_id=1, source_target_pairs={{0,17},{1,18},{2,19},{3,20},{4,21},{5,22},{6,23},{7,24},{8,25},{9,... | collective-permute-start | bytes 589832
  2129.9 54.4 %collective-permute-start.15 = (f32[16,3072]{1,0:T(8,128)}, f32[16,3072]{1,0:T(8,128)}, u32[]{:S(2)}, u32[]{:S(2)}) collective-permute-start(f32[16,3072]{1,0:T(8,128)} %fusion.2), channel_id=1, source_target_pairs={{0,16},{1,17},{2,18},{3,19},{4,20},{5,21},{6,22},{7,23},{8,24},{9,... | collective-permute-start | bytes 589832
  2165.4 209.2 %all-to-all-start.6 = ((bf16[8,2,36864]{2,1,0:T(2,128)(2,1)}), bf16[8,2,36864]{2,1,0:T(2,128)(2,1)}, u32[]{:S(2)}, u32[]{:S(2)}) async-start(bf16[8,2,36864]{2,1,0:T(2,128)(2,1)} %reshape.376), calls=%async_computation.6 | async-start | bytes 2359296 | tf_op jit(solution)/shard_map/all_to_all | solution.py:118
  2172.7 28.7 %collective-permute-start.14 = (f32[16,3072]{1,0:T(8,128)S(1)}, f32[16,3072]{1,0:T(8,128)S(1)}, u32[]{:S(2)}, u32[]{:S(2)}) collective-permute-start(f32[16,3072]{1,0:T(8,128)S(1)} %copy-done.10), channel_id=1, source_target_pairs={{0,15},{1,16},{2,17},{3,18},{4,19},{5,20},{6,21},{7,22},{8,23},{9,... | collective-permute-start | bytes 589832
  2174.7 28.6 %collective-permute-start.13 = (f32[16,3072]{1,0:T(8,128)S(1)}, f32[16,3072]{1,0:T(8,128)S(1)}, u32[]{:S(2)}, u32[]{:S(2)}) collective-permute-start(f32[16,3072]{1,0:T(8,128)S(1)} %copy-done.10), channel_id=1, source_target_pairs={{0,14},{1,15},{2,16},{3,17},{4,18},{5,19},{6,20},{7,21},{8,22},{9,... | collective-permute-start | bytes 589832
  2176.8 28.4 %collective-permute-start.12 = (f32[16,3072]{1,0:T(8,128)S(1)}, f32[16,3072]{1,0:T(8,128)S(1)}, u32[]{:S(2)}, u32[]{:S(2)}) collective-permute-start(f32[16,3072]{1,0:T(8,128)S(1)} %copy-done.10), channel_id=1, source_target_pairs={{0,13},{1,14},{2,15},{3,16},{4,17},{5,18},{6,19},{7,20},{8,21},{9,... | collective-permute-start | bytes 589832
  2179.4 28.3 %collective-permute-start.11 = (f32[16,3072]{1,0:T(8,128)S(1)}, f32[16,3072]{1,0:T(8,128)S(1)}, u32[]{:S(2)}, u32[]{:S(2)}) collective-permute-start(f32[16,3072]{1,0:T(8,128)S(1)} %copy-done.10), channel_id=1, source_target_pairs={{0,12},{1,13},{2,14},{3,15},{4,16},{5,17},{6,18},{7,19},{8,20},{9,... | collective-permute-start | bytes 589832
  2184.3 32.5 %collective-permute-start.10 = (f32[16,3072]{1,0:T(8,128)S(1)}, f32[16,3072]{1,0:T(8,128)S(1)}, u32[]{:S(2)}, u32[]{:S(2)}) collective-permute-start(f32[16,3072]{1,0:T(8,128)S(1)} %copy-done.10), channel_id=1, source_target_pairs={{0,11},{1,12},{2,13},{3,14},{4,15},{5,16},{6,17},{7,18},{8,19},{9,... | collective-permute-start | bytes 589832
  2207.6 29.3 %collective-permute-start.6 = (f32[16,3072]{1,0:T(8,128)S(1)}, f32[16,3072]{1,0:T(8,128)S(1)}, u32[]{:S(2)}, u32[]{:S(2)}) collective-permute-start(f32[16,3072]{1,0:T(8,128)S(1)} %copy-done.10), channel_id=1, source_target_pairs={{0,7},{1,8},{2,9},{3,10},{4,11},{5,12},{6,13},{7,14},{8,15},{9,16}... | collective-permute-start | bytes 589832
  2216.8 30.9 %collective-permute-start.5 = (f32[16,3072]{1,0:T(8,128)S(1)}, f32[16,3072]{1,0:T(8,128)S(1)}, u32[]{:S(2)}, u32[]{:S(2)}) collective-permute-start(f32[16,3072]{1,0:T(8,128)S(1)} %copy-done.10), channel_id=1, source_target_pairs={{0,6},{1,7},{2,8},{3,9},{4,10},{5,11},{6,12},{7,13},{8,14},{9,15},... | collective-permute-start | bytes 589832
  2220.0 29.8 %collective-permute-start.4 = (f32[16,3072]{1,0:T(8,128)S(1)}, f32[16,3072]{1,0:T(8,128)}, u32[]{:S(2)}, u32[]{:S(2)}) collective-permute-start(f32[16,3072]{1,0:T(8,128)S(1)} %copy-done.10), channel_id=1, source_target_pairs={{0,5},{1,6},{2,7},{3,8},{4,9},{5,10},{6,11},{7,12},{8,13},{9,14},{... | collective-permute-start | bytes 589832
  (151 other events, 1264.7 us)
Sparse Core Ops, SparseCore 0:
  90.0 57.7 all-gather.1
where the time goes:
time: 2440 us; the launch traced here: 2400 us
  local copies, waits for them, and re-layouts  811 us (33%)
  blocking collectives  550 us (23%)
  other arithmetic  421 us (17%)
  matrix products  368 us (15%)
  starting transfers between devices  206 us (8%)
    unnamed x1, blocking collectives  550 us
    unnamed x61, local copies, waits for them, and re-layouts  192 us
    dot_general x72, matrix products, one_block(): jnp.dot(probs.astype(jnp.bfloat16), values, preferred_element_type=jnp.fl...  159 us
    unnamed x32, starting transfers between devices  147 us
    gather x72, local copies, waits for them, and re-layouts, one_block(): keys = key_blocks[ids].reshape(slots * width, hdim).astype(jnp.bfloat16)  139 us
    scatter-add x48, other arithmetic, one_block(): keys = key_blocks[ids].reshape(slots * width, hdim).astype(jnp.bfloat16)  124 us
    unnamed x9, other arithmetic  121 us
    dot_general x72, matrix products, one_block(): lax.dot_general(q_rows.astype(jnp.bfloat16), keys, (((1,), (1,)), ((), ()...  121 us
  transfers between devices with their start and end apart: 41, of which 4 were waited for; matrix products, arithmetic and copies ran while one was open for 50% of the time, Pallas kernels for 0%

commit v1 on v0

v1 whole, which is shorter than its diff:
```python
import functools

import jax
import jax.numpy as jnp
from jax import lax
from jax.experimental import pallas as pl
from jax.experimental.pallas import tpu as pltpu
from jax.sharding import PartitionSpec as P

HDIM = 64
BLK = 128
NT = (((1,), (1,)), ((), ()))
NN = (((1,), (0,)), ((), ()))
TN = (((0,), (0,)), ((), ()))
BF16 = jnp.bfloat16
F32 = jnp.float32


def join(a, b, head):
    cols = slice(head * HDIM, (head + 1) * HDIM)
    return jnp.concatenate([a[:, cols], b[:, cols]], axis=1)


def pack_kernel(a_ref, b_ref, out_ref):
    a, b = a_ref[...], b_ref[...]
    for peer in range(out_ref.shape[0]):
        for j in range(out_ref.shape[1]):
            out_ref[peer, j] = join(a, b, peer * out_ref.shape[1] + j)


def project_kernel(dy_ref, w_ref, q_ref, out_ref):
    d = lax.dot_general(dy_ref[...], w_ref[...], NT, preferred_element_type=F32).astype(BF16)
    q = q_ref[...]
    for peer in range(out_ref.shape[0]):
        for j in range(out_ref.shape[1]):
            out_ref[peer, j] = join(q, d, peer * out_ref.shape[1] + j)


def unpack_kernel(x_ref, a_ref, b_ref):
    peers, per, _, _ = x_ref.shape
    parts = [x_ref[p, j] for p in range(peers) for j in range(per)]
    a_ref[...] = jnp.concatenate([x[:, :HDIM] for x in parts], axis=1)
    b_ref[...] = jnp.concatenate([x[:, HDIM:] for x in parts], axis=1)


def weight_kernel(x_ref, dy_ref, a_ref, gw_ref):
    peers, per, _, _ = x_ref.shape
    parts = [x_ref[p, j] for p in range(peers) for j in range(per)]
    a_ref[...] = jnp.concatenate([x[:, :HDIM] for x in parts], axis=1)
    attn = jnp.concatenate([x[:, HDIM:] for x in parts], axis=1)
    gw_ref[...] = lax.dot_general(attn, dy_ref[...], TN, preferred_element_type=F32).astype(BF16)


def attn_block(n, h, i, idx_ref, qd_ref, kv_ref, kvt_ref, acc_ref, out_ref):
    per = qd_ref.shape[2] // BLK

    def rows(block):
        return pl.ds(pl.multiple_of(block * BLK, BLK), BLK)

    qd = qd_ref[i // per, h, rows(i % per), :]
    left = lax.broadcasted_iota(jnp.int32, (BLK, BLK), 1) < HDIM
    qs = jnp.where(left, qd * BF16(HDIM**-0.5), jnp.zeros_like(qd))
    do = jnp.where(left, jnp.zeros_like(qd), qd)
    both = jnp.concatenate([qs, do], axis=0)
    ids = [idx_ref[h, i, m] for m in range(n)]
    sd = [
        lax.dot_general(
            kv_ref[b // per, h, rows(b % per), :], both, NT, preferred_element_type=F32
        )
        for b in ids
    ]
    s = [x[:, :BLK] for x in sd]
    dp = [x[:, BLK:] for x in sd]
    top = jnp.max(functools.reduce(jnp.maximum, s), axis=0, keepdims=True)
    w = [jnp.exp(x - top) for x in s]
    inv = 1.0 / jnp.sum(functools.reduce(jnp.add, w), axis=0, keepdims=True)
    p = [x * inv for x in w]
    delta = jnp.sum(
        functools.reduce(jnp.add, [a * b for a, b in zip(p, dp)]), axis=0, keepdims=True
    )
    ds = [a * (b - delta) for a, b in zip(p, dp)]
    dsp = [jnp.concatenate([a.astype(BF16), b.astype(BF16)], axis=1) for a, b in zip(ds, p)]
    for m in range(n):
        acc_ref[h, rows(ids[m]), :] += lax.dot_general(
            dsp[m], both, NN, preferred_element_type=F32
        )
    kt = jnp.concatenate([kvt_ref[h, :, rows(b)] for b in ids], axis=1)
    o = lax.dot_general(kt, jnp.concatenate(dsp, axis=0), NN, preferred_element_type=F32)
    upper = lax.broadcasted_iota(jnp.int32, (BLK, BLK), 0) < HDIM
    res = jnp.where(upper, o[:, :BLK] * HDIM**-0.5, o[:, BLK:])
    out_ref[i // per, h, rows(i % per), :] = res.T.astype(BF16)


def attn_kernel(idx_ref, cnt_ref, qd_ref, kv_ref, out_ref, dkv_ref, kvt_ref, acc_ref):
    peers, heads, per, _ = qd_ref.shape
    per = per // BLK
    blocks = peers * per
    slots = idx_ref.shape[2]

    def rows(block):
        return pl.ds(pl.multiple_of(block * BLK, BLK), BLK)

    @pl.loop(0, heads)
    def _(h):
        @pl.loop(0, blocks)
        def _(j):
            kvt_ref[h, :, rows(j)] = kv_ref[j // per, h, rows(j % per), :].T
            acc_ref[h, rows(j), :] = jnp.zeros((BLK, BLK), F32)

        @pl.loop(0, blocks)
        def _(i):
            c = cnt_ref[h, i]
            for n in range(1, slots + 1):

                @pl.when(c == n)
                def _():
                    attn_block(n, h, i, idx_ref, qd_ref, kv_ref, kvt_ref, acc_ref, out_ref)

        @pl.loop(0, blocks)
        def _(j):
            dkv_ref[j // per, h, rows(j % per), :] = acc_ref[h, rows(j), :].astype(BF16)


V = pl.BlockSpec(memory_space=pltpu.VMEM)
S = pl.BlockSpec(memory_space=pltpu.SMEM)


def cost(flops, *arrays):
    return pl.CostEstimate(
        flops=flops, bytes_accessed=sum(a.size * a.dtype.itemsize for a in arrays), transcendentals=0
    )


def attention(idx, cnt, qd, kv):
    peers, heads, per, _ = qd.shape
    seq = peers * per
    out = jax.ShapeDtypeStruct(qd.shape, BF16)
    return pl.pallas_call(
        attn_kernel,
        out_shape=(out, out),
        in_specs=[S, S, V, V],
        out_specs=(V, V),
        scratch_shapes=[
            pltpu.VMEM((heads, BLK, seq), BF16),
            pltpu.VMEM((heads, seq, BLK), F32),
        ],
        compiler_params=pltpu.CompilerParams(vmem_limit_bytes=48 * 2**20),
        cost_estimate=cost(60_000_000_000, qd, kv, out, out),
        name="attention",
    )(idx, cnt, qd, kv)


def wide(rows, cols, pos=1):
    return pl.BlockSpec((rows, cols), (lambda t: (0, t)) if pos else (lambda t: (t, 0)))


def local(query, key_states, value_states, grad_out, w_out, block_index, block_count):
    rows, hd = query.shape[1:]
    depth = grad_out.shape[2]
    n_seq, n_dp = lax.axis_size("seq"), lax.axis_size("dp")
    heads = hd // HDIM
    per = heads // n_seq
    tiles = n_seq // 2
    cols = hd // tiles
    packed = jax.ShapeDtypeStruct((n_seq, per, rows, BLK), BF16)
    pairs = pl.BlockSpec((2, per, rows, BLK), lambda t: (t, 0, 0, 0))
    flat = jax.ShapeDtypeStruct((rows, hd), BF16)
    big = pltpu.CompilerParams(vmem_limit_bytes=48 * 2**20)
    q, k, v, dy = query[0], key_states[0], value_states[0], grad_out[0]

    def swap(x):
        return lax.all_to_all(x, "seq", split_axis=0, concat_axis=0, tiled=True)

    w_all = lax.all_gather(w_out, "dp", axis=0, tiled=True)
    kv = pl.pallas_call(
        pack_kernel, out_shape=packed, grid=(tiles,), in_specs=[wide(rows, cols)] * 2, out_specs=pairs,
        cost_estimate=cost(0, k, v, packed), name="pack",
    )(k, v)
    kv = swap(kv)
    qd = pl.pallas_call(
        project_kernel, out_shape=packed, grid=(tiles,),
        in_specs=[pl.BlockSpec((rows, depth), lambda t: (0, 0)), wide(cols, depth, 0), wide(rows, cols)],
        out_specs=pairs, compiler_params=big,
        cost_estimate=cost(2 * rows * depth * hd, dy, w_all, q, packed), name="project",
    )(dy, w_all, q)
    qd = swap(qd)
    first = lax.axis_index("seq") * per
    idx = lax.dynamic_slice_in_dim(block_index, first, per, 0)
    cnt = lax.dynamic_slice_in_dim(block_count, first, per, 0)
    odq, dkv = attention(idx, cnt, qd, kv)
    odq, dkv = swap(odq), swap(dkv)
    dq, gw = pl.pallas_call(
        weight_kernel, out_shape=(flat, jax.ShapeDtypeStruct((hd, depth), BF16)), grid=(tiles,),
        in_specs=[pairs, pl.BlockSpec((rows, depth), lambda t: (0, 0))],
        out_specs=(wide(rows, cols), wide(cols, depth, 0)), compiler_params=big,
        cost_estimate=cost(2 * rows * depth * hd, dy, w_all, packed), name="weight",
    )(odq, dy)
    dk, dv = pl.pallas_call(
        unpack_kernel, out_shape=(flat, flat), grid=(tiles,), in_specs=[pairs],
        out_specs=(wide(rows, cols),) * 2, cost_estimate=cost(0, k, v, packed), name="unpack",
    )(dkv)
    gw = lax.psum_scatter(gw.reshape(n_seq, hd // n_seq, depth), "seq", scatter_dimension=0)
    gw = lax.psum_scatter(
        gw.reshape(n_dp, hd // n_seq // n_dp, depth), "dp", scatter_dimension=0
    )
    scale = float(rows * n_seq * n_dp) ** (-0.5)
    return dq[None], dk[None], dv[None], gw.astype(F32) * scale


def solution(mesh):
    tok = P("dp", "seq", None)
    return jax.shard_map(
        local,
        mesh=mesh,
        in_specs=(tok, tok, tok, tok, P("dp", None), P(), P()),
        out_specs=(tok, tok, tok, P(("seq", "dp"), None)),
        check_vma=False,
    )
```

time: 2440 us -> 471 us (0.19); the launches traced: 2400 us -> 464 us
  local copies, waits for them, and re-layouts: 811 us -> 4.41 us
  blocking collectives: 550 us -> 74.7 us
  other arithmetic: 421 us -> 1.58 us
  matrix products: 368 us -> 0 us
  waiting for transfers between devices: 22.2 us -> 259 us
  starting transfers between devices: 206 us -> 14.6 us
  Pallas kernels: 0 us -> 96.4 us
    unnamed x1 -> x0, blocking collectives: 550 us -> none
    dot_general x146 -> x0, matrix products: 297 us -> none  [the longest x72 159 us: one_block(): jnp.dot(probs.astype(jnp.bfloat16), values, preferred_element_type=jnp.fl...]
    gather x120 -> x0, local copies, waits for them, and re-layouts: 255 us -> none  [the longest x72 139 us: one_block(): keys = key_blocks[ids].reshape(slots * width, hdim).astype(jnp.bfloat16)]
    scatter-add x72 -> x0, other arithmetic: 245 us -> none  [the longest x48 124 us: one_block(): keys = key_blocks[ids].reshape(slots * width, hdim).astype(jnp.bfloat16)]
    unnamed x61 -> x9, local copies, waits for them, and re-layouts: 192 us -> 1.36 us
    reshape x149 -> x0, local copies, waits for them, and re-layouts: 161 us -> none  [the longest x72 75 us: one_block(): keys = key_blocks[ids].reshape(slots * width, hdim).astype(jnp.bfloat16)]
    reduce_scatter x0 -> x2, waiting for transfers between devices: none -> 155 us  [the longest x1 123 us: local(): lax.psum_scatter(gw.reshape(n_seq, hd // n_seq, depth), 'seq', scatter_di...]
    unnamed x32 -> x0, starting transfers between devices: 147 us -> none
  transfers between devices with their start and end apart: 41 -> 5, of which waited for: 4 -> 4; matrix products, arithmetic and copies ran while one was open for 50% -> 0% of each run, Pallas kernels for 0% -> 4%
where the time goes in v1:
time: 471 us; the launch traced here: 464 us
  waiting for transfers between devices  259 us (55%)
  Pallas kernels  96.4 us (20%)
  blocking collectives  74.7 us (16%)
  starting transfers between devices  14.6 us (3%)
  between operations  13.8 us (3%)
    reduce_scatter x1, waiting for transfers between devices, local(): lax.psum_scatter(gw.reshape(n_seq, hd // n_seq, depth), 'seq', scatter_di...  123 us
    all_to_all x2, blocking collectives, swap(): return lax.all_to_all(x, 'seq', split_axis=0, concat_axis=0, tiled=True)  74.7 us
    all_gather x1, waiting for transfers between devices, local(): w_all = lax.all_gather(w_out, 'dp', axis=0, tiled=True)  72.9 us
    pallas_call x1, Pallas kernels, attention(): pl.pallas_call(attn_kernel, out_shape=(out, out), in_specs=[S, S, V, V],...  71.2 us
    reduce_scatter x1, waiting for transfers between devices, local(): lax.psum_scatter(gw.reshape(n_dp, hd // n_seq // n_dp, depth), 'dp', scat...  31.4 us
    all_to_all x2, waiting for transfers between devices, swap(): return lax.all_to_all(x, 'seq', split_axis=0, concat_axis=0, tiled=True)  30.1 us
    all_to_all x2, starting transfers between devices, swap(): return lax.all_to_all(x, 'seq', split_axis=0, concat_axis=0, tiled=True)  14.5 us
  transfers between devices with their start and end apart: 5, of which 4 were waited for; matrix products, arithmetic and copies ran while one was open for 0% of the time, Pallas kernels for 4%

profile of v1, /device:TPU:116, one launch (start us, length us, event | category | flops | bytes accessed | tf_op | source)
XLA Modules:
  0.0 464.1 jit_solution(2924805793102568368)
XLA Ops:
  7.2 0.0 copy-start
  7.2 0.0 all-gather.2.cloned.1.call-start
  7.2 0.7 all-gather.2.cloned.1.call-update
  7.9 4.3 pack.1
  12.2 7.3 %all-to-all-start.1 = ((bf16[8,3,384,128]{3,2,1,0:T(8,128)(2,1)}), bf16[8,3,384,128]{3,2,1,0:T(8,128)(2,1)}, u32[]{:S(2)}, u32[]{:S(2)}) async-start(bf16[8,3,384,128]{3,2,1,0:T(8,128)(2,1)} %pack.1), calls=%async_computation.1 | async-start | bytes 4718592 | tf_op jit(solution)/shard_map/all_to_all | solution.py:172
  19.5 72.9 %all-gather.2.cloned.1.call-done.w_ref = bf16[1536,3072]{1,0:T(8,128)(2,1)} async-done(((bf16[96,3072]{1,0:T(8,128)(2,1)}), bf16[1536,3072]{1,0:T(8,128)(2,1)}) %all-gather.2.cloned.1.call-update) | async-done | bytes 9437200 | tf_op jit(solution)/shard_map/all_gather | solution.py:174
  92.4 1.3 copy-done.3
  93.7 9.0 %project.1 = bf16[8,3,384,128]{3,2,1,0:T(8,128)(2,1)} custom-call(bf16[384,3072]{1,0:T(8,128)(2,1)S(1)} %bitcast.10, bf16[1536,3072]{1,0:T(8,128)(2,1)} %all-gather.2.cloned.1.call-done.w_ref, bf16[384,1536]{1,0:T(8,128)(2,1)S(1)} %bitcast.12), custom_call_target="tpu_custom_call" | custom-call | flops 3623878656 | bytes 15335424 | tf_op jit(solution)/shard_map/project/pallas_call | solution.py:180
  102.6 7.2 %all-to-all-start = ((bf16[8,3,384,128]{3,2,1,0:T(8,128)(2,1)}), bf16[8,3,384,128]{3,2,1,0:T(8,128)(2,1)}, u32[]{:S(2)}, u32[]{:S(2)}) async-start(bf16[8,3,384,128]{3,2,1,0:T(8,128)(2,1)} %project.1), calls=%async_computation | async-start | bytes 4718592 | tf_op jit(solution)/shard_map/all_to_all | solution.py:172
  109.9 0.1 copy.13.idx_ref
  109.9 0.7 constant_dynamic-slice_fusion.cnt_ref
  110.6 30.1 %all-to-all-done.qd_ref = bf16[8,3,384,128]{3,2,1,0:T(8,128)(2,1)} async-done(((bf16[8,3,384,128]{3,2,1,0:T(8,128)(2,1)}), bf16[8,3,384,128]{3,2,1,0:T(8,128)(2,1)}, u32[]{:S(2)}, u32[]{:S(2)}) %all-to-all-start) | async-done | bytes 2359328 | tf_op jit(solution)/shard_map/all_to_all | solution.py:172
  140.7 71.2 %attention.1 = (bf16[8,3,384,128]{3,2,1,0:T(8,128)(2,1)S(1)}, bf16[8,3,384,128]{3,2,1,0:T(8,128)(2,1)S(1)}) custom-call(s32[3,24,8]{2,1,0:T(8,128)S(1)} %copy.13.idx_ref, s32[3,24]{1,0:T(4,128)S(1)} %constant_dynamic-slice_fusion.cnt_ref, bf16[8,3,384,128]{3,2,1,0:T(8,128)(2,1)} %all-to-all-done.qd_ref, bf16[8,3,384,128]{3,2,1,0:T(8,128)(2,1)} %all-to-all-done.1.kv_ref), custom_call_target="tpu_custom_call" | custom-call | flops 60000002048 | bytes 9437184 | tf_op jit(solution)/shard_map/attention/pallas_call | solution.py:138
  211.9 38.6 %all_to_all.20.x_ref = bf16[8,3,384,128]{3,2,1,0:T(8,128)(2,1)S(1)} all-to-all(bf16[8,3,384,128]{3,2,1,0:T(8,128)(2,1)S(1)} %get-tuple-element.10), channel_id=1, replica_groups=mesh['dp'=16,'seq'=8] {'seq'}, dimensions={0} | all-to-all | bytes 4718592 | tf_op jit(solution)/shard_map/all_to_all | solution.py:172
  250.6 7.9 %weight.1 = (bf16[384,1536]{1,0:T(8,128)(2,1)}, bf16[1536,3072]{1,0:T(8,128)(2,1)}) custom-call(bf16[8,3,384,128]{3,2,1,0:T(8,128)(2,1)S(1)} %all_to_all.20.x_ref, bf16[384,3072]{1,0:T(8,128)(2,1)S(1)} %bitcast.11), custom_call_target="tpu_custom_call" | custom-call | flops 3623878656 | bytes 14155776 | tf_op jit(solution)/shard_map/weight/pallas_call | solution.py:192
  258.5 0.0 reduce-scatter.3.cloned.1.call-update
  258.5 0.0 reduce-scatter.5.cloned.1.call-start
  258.6 123.4 %reduce-scatter.3.cloned.1.call-done = bf16[1,192,3072]{2,1,0:T(8,128)(2,1)} async-done(((bf16[8,192,3072]{2,1,0:T(8,128)(2,1)}), bf16[1,192,3072]{2,1,0:T(8,128)(2,1)}) %reduce-scatter.3.cloned.1.call-update) | async-done | bytes 1179664 | tf_op jit(solution)/shard_map/reduce_scatter | solution.py:202
  382.0 2.3 reshape_reduce_scatter.3
  384.3 0.0 reduce-scatter.5.cloned.1.call-update
  384.3 36.1 %all_to_all.21.x_ref = bf16[8,3,384,128]{3,2,1,0:T(8,128)(2,1)} all-to-all(bf16[8,3,384,128]{3,2,1,0:T(8,128)(2,1)S(1)} %get-tuple-element.12), channel_id=1, replica_groups=mesh['dp'=16,'seq'=8] {'seq'}, dimensions={0} | all-to-all | bytes 4718592 | tf_op jit(solution)/shard_map/all_to_all | solution.py:172
  420.4 4.1 unpack.1
  424.5 31.4 %reduce-scatter.5.cloned.1.call-done = bf16[1,12,3072]{2,1,0:T(8,128)(2,1)} async-done(((bf16[16,12,3072]{2,1,0:T(8,128)(2,1)}), bf16[1,12,3072]{2,1,0:T(8,128)(2,1)}) %reduce-scatter.5.cloned.1.call-update) | async-done | bytes 73744 | tf_op jit(solution)/shard_map/reduce_scatter | solution.py:203
  455.9 1.6 multiply_bitcast_fusion
  (9 shorter events, 0.0 us)
Async XLA Ops:
  7.2 102.7 %copy-start = (s32[24,24,8]{1,2,0:T(8,128)S(1)}, s32[24,24,8]{1,2,0:T(8,128)}, u32[]{:S(2)}) copy-start(s32[24,24,8]{1,2,0:T(8,128)} %param.12) | copy-start | bytes 55300
  7.2 85.2 %all-gather.2.cloned.1.call-start = ((), (), s32[]{:S(2)}) async-start(), calls=%async_computation.6 | async-start | bytes 10027008 | tf_op jit(solution)/shard_map/all_gather | solution.py:174
  12.2 80.2 %copy-start.1 = (bf16[1,384,3072]{2,1,0:T(8,128)(2,1)S(1)}, bf16[1,384,3072]{2,1,0:T(8,128)(2,1)}, u32[]{:S(2)}) copy-start(bf16[1,384,3072]{2,1,0:T(8,128)(2,1)} %param.10) | copy-start | bytes 7077892
  12.2 90.4 %all-to-all-start.1 = ((bf16[8,3,384,128]{3,2,1,0:T(8,128)(2,1)}), bf16[8,3,384,128]{3,2,1,0:T(8,128)(2,1)}, u32[]{:S(2)}, u32[]{:S(2)}) async-start(bf16[8,3,384,128]{3,2,1,0:T(8,128)(2,1)} %pack.1), calls=%async_computation.1 | async-start | bytes 4718592 | tf_op jit(solution)/shard_map/all_to_all | solution.py:172
  92.4 1.3 copy-start.3
  102.6 38.1 %all-to-all-start = ((bf16[8,3,384,128]{3,2,1,0:T(8,128)(2,1)}), bf16[8,3,384,128]{3,2,1,0:T(8,128)(2,1)}, u32[]{:S(2)}, u32[]{:S(2)}) async-start(bf16[8,3,384,128]{3,2,1,0:T(8,128)(2,1)} %project.1), calls=%async_computation | async-start | bytes 4718592 | tf_op jit(solution)/shard_map/all_to_all | solution.py:172
  109.8 272.1 %reduce-scatter.3.cloned.1.call-start = ((), (), s32[]{:S(2)}) async-start(), calls=%async_computation.7 | async-start | bytes 10616832 | tf_op jit(solution)/shard_map/reduce_scatter | solution.py:202
  211.9 38.6 %copy-start.2 = (bf16[1,384,3072]{2,1,0:T(8,128)(2,1)S(1)}, bf16[1,384,3072]{2,1,0:T(8,128)(2,1)}, u32[]{:S(2)}) copy-start(bf16[1,384,3072]{2,1,0:T(8,128)(2,1)} %param.10) | copy-start | bytes 7077892
  258.5 197.4 %reduce-scatter.5.cloned.1.call-start = ((), (), s32[]{:S(2)}) async-start(), calls=%async_computation.8 | async-start | bytes 1671168 | tf_op jit(solution)/shard_map/reduce_scatter | solution.py:203
Sparse Core Ops, SparseCore 0:
  9.7 82.6 all-gather.1
  258.6 123.3 reduce-scatter.2
  384.5 71.3 reduce-scatter.4

commit v2 on v1

v2 whole, which is shorter than its diff:
```python
import functools

import jax
import jax.numpy as jnp
from jax import lax
from jax.experimental import pallas as pl
from jax.experimental.pallas import tpu as pltpu
from jax.sharding import PartitionSpec as P

HDIM = 64
BLK = 128
NT = (((1,), (1,)), ((), ()))
NN = (((1,), (0,)), ((), ()))
TN = (((0,), (0,)), ((), ()))
BF16 = jnp.bfloat16
F32 = jnp.float32
MESH = pl.DeviceIdType.MESH
TB = 3
Q_AT = 1152


def pack_kernel(q_ref, k_ref, v_ref, out_ref):
    k, v = k_ref[...], v_ref[...]
    rows = k.shape[0]
    qt = q_ref[...].T
    feats = qt.shape[0] // 2
    for peer in range(2):
        for j in range(feats // HDIM):
            cols = slice(peer * feats + j * HDIM, peer * feats + (j + 1) * HDIM)
            out_ref[peer, j * rows : (j + 1) * rows] = jnp.concatenate([k[:, cols], v[:, cols]], axis=1)
        for t in range(rows // BLK):
            at = Q_AT + t * feats
            out_ref[peer, at : at + feats] = qt[peer * feats : (peer + 1) * feats, t * BLK : (t + 1) * BLK]


def project_kernel(dy_ref, w_ref, out_ref):
    d = lax.dot_general(w_ref[...], dy_ref[...], NT, preferred_element_type=F32).astype(BF16)
    feats = d.shape[0] // 2
    for peer in range(2):
        for t in range(d.shape[1] // BLK):
            out_ref[peer, t * feats : (t + 1) * feats] = d[
                peer * feats : (peer + 1) * feats, t * BLK : (t + 1) * BLK
            ]


def unpack_kernel(x_ref, q_ref, k_ref, v_ref):
    rows = q_ref.shape[0]
    feats = q_ref.shape[1] // 2
    ks, vs, qs = [], [], []
    for peer in range(2):
        for j in range(feats // HDIM):
            x = x_ref[peer, j * rows : (j + 1) * rows]
            ks.append(x[:, :HDIM])
            vs.append(x[:, HDIM:])
        qs.append(
            jnp.concatenate(
                [x_ref[peer, Q_AT + t * feats : Q_AT + (t + 1) * feats] for t in range(rows // BLK)], axis=1
            )
        )
    q_ref[...] = jnp.concatenate(qs, axis=0).T
    k_ref[...] = jnp.concatenate(ks, axis=1)
    v_ref[...] = jnp.concatenate(vs, axis=1)


def attn_block(n, h, i, idx_ref, x_ref, d_ref, kvt_ref, acc_ref, at_ref, g_ref):
    tb = TB
    feats = d_ref.shape[1] // tb
    per = tb * BLK

    def key_rows(b):
        return pl.ds(pl.multiple_of(h * per + (b % tb) * BLK, BLK), BLK)

    def seq_rows(b):
        return pl.ds(pl.multiple_of(b * BLK, BLK), BLK)

    at = pl.multiple_of((i % tb) * feats + h * HDIM, HDIM)
    qt = x_ref[i // tb, pl.ds(pl.multiple_of(Q_AT + at, HDIM), HDIM), :] * BF16(HDIM**-0.5)
    dt = d_ref[i // tb, pl.ds(at, HDIM), :]
    zero = jnp.zeros_like(qt)
    both = jnp.concatenate(
        [jnp.concatenate([qt, zero], axis=1), jnp.concatenate([zero, dt], axis=1)], axis=0
    )
    ids = [idx_ref[h, i, m] for m in range(n)]
    sd = [
        lax.dot_general(x_ref[b // tb, key_rows(b), :], both, NN, preferred_element_type=F32)
        for b in ids
    ]
    s = [x[:, :BLK] for x in sd]
    dp = [x[:, BLK:] for x in sd]
    top = jnp.max(functools.reduce(jnp.maximum, s), axis=0, keepdims=True)
    w = [jnp.exp(x - top) for x in s]
    inv = 1.0 / jnp.sum(functools.reduce(jnp.add, w), axis=0, keepdims=True)
    p = [x * inv for x in w]
    delta = jnp.sum(
        functools.reduce(jnp.add, [a * b for a, b in zip(p, dp)]), axis=0, keepdims=True
    )
    ds = [a * (b - delta) for a, b in zip(p, dp)]
    dsp = [jnp.concatenate([a.astype(BF16), b.astype(BF16)], axis=1) for a, b in zip(ds, p)]
    for m in range(n):
        acc_ref[h, seq_rows(ids[m]), :] += lax.dot_general(
            dsp[m], both, NT, preferred_element_type=F32
        )
    kt = jnp.concatenate([kvt_ref[h, :, seq_rows(b)] for b in ids], axis=1)
    o = lax.dot_general(kt, jnp.concatenate(dsp, axis=0), NN, preferred_element_type=F32)
    g_ref[i // tb, pl.ds(pl.multiple_of(Q_AT + at, HDIM), HDIM), :] = (
        o[:HDIM, :BLK] * HDIM**-0.5
    ).astype(BF16)
    at_ref[i // tb, pl.ds(at, HDIM), :] = o[HDIM:, BLK:].astype(BF16)


def attn_kernel(idx_ref, cnt_ref, x_ref, d_ref, at_ref, g_ref, kvt_ref, acc_ref):
    heads, blocks = cnt_ref.shape
    tb = blocks // x_ref.shape[0]
    slots = idx_ref.shape[2]

    def key_rows(h, b):
        return pl.ds(pl.multiple_of(h * tb * BLK + (b % tb) * BLK, BLK), BLK)

    def seq_rows(b):
        return pl.ds(pl.multiple_of(b * BLK, BLK), BLK)

    @pl.loop(0, heads)
    def _(h):
        @pl.loop(0, blocks)
        def _(j):
            kvt_ref[h, :, seq_rows(j)] = x_ref[j // tb, key_rows(h, j), :].T
            acc_ref[h, seq_rows(j), :] = jnp.zeros((BLK, BLK), F32)

        @pl.loop(0, blocks)
        def _(i):
            c = cnt_ref[h, i]
            for n in range(1, slots + 1):

                @pl.when(c == n)
                def _():
                    attn_block(n, h, i, idx_ref, x_ref, d_ref, kvt_ref, acc_ref, at_ref, g_ref)

        @pl.loop(0, blocks)
        def _(j):
            g_ref[j // tb, key_rows(h, j), :] = acc_ref[h, seq_rows(j), :].astype(BF16)


def back_kernel(scale, at_ref, g_ref, dy_ref, gr_ref, gw_ref, atr, dyx, part, ring, plane, total, half, other,
                at_s, at_r, fw_s, fw_r, dy_s, dy_r, g_s, g_r, z_s, z_r, p_s, p_r, o_s, o_r, loc):
    dp, me = lax.axis_index("dp"), lax.axis_index("seq")
    core, zz, lo = dp % 2, (dp // 2) % 4, dp // 8
    sib = dp + 1 - 2 * core
    tiles, nz, slabs, srows, tcols = part.shape
    peers = at_ref.shape[0]
    feats = at_ref.shape[1] // TB
    tb = TB
    cols = dyx.shape[2]
    my = me * 2 + lo

    def at_z(k):
        return lo * 8 + lax.rem(zz + k + nz, nz) * 2 + core

    def plane_peer(k):
        j = lax.rem(my + k, slabs)
        return j, {"dp": (j % 2) * 8 + zz * 2 + core, "seq": j // 2}

    bar = pltpu.get_barrier_semaphore()

    def hello(where):
        pl.semaphore_signal(bar, inc=1, device_id=where, device_id_type=MESH)

    @pl.loop(1, slabs)
    def _(k):
        hello(plane_peer(k)[1])

    hello({"dp": sib})
    hello({"dp": at_z(1)})
    hello({"dp": at_z(-1)})
    pl.semaphore_wait(bar, slabs + 2)

    def remote(src, dst, ssem, rsem, where):
        return pltpu.make_async_remote_copy(
            src_ref=src, dst_ref=dst, send_sem=ssem, recv_sem=rsem, device_id=where, device_id_type=MESH
        )

    def at_copy(k):
        p = lax.rem(me + k, peers)
        return remote(at_ref.at[p], atr.at[0, me], at_s.at[k], at_r.at[k], {"seq": p})

    @pl.loop(1, peers)
    def _(k):
        at_copy(k).start()

    mine = pl.ds(pl.multiple_of(core * cols, BLK), cols)
    theirs = pl.ds(pl.multiple_of((1 - core) * cols, BLK), cols)
    dy_copy = remote(dy_ref.at[:, theirs], dyx.at[1], dy_s, dy_r, {"dp": sib})
    dy_copy.start()
    own_dy = pltpu.make_async_copy(dy_ref.at[:, mine], dyx.at[0], loc.at[0])
    own_dy.start()
    own_at = pltpu.make_async_copy(at_ref.at[me], atr.at[0, me], loc.at[1])
    own_at.start()
    own_g = pltpu.make_async_copy(g_ref.at[me], gr_ref.at[me], loc.at[2])
    own_g.start()

    def forward(s, k):
        return remote(atr.at[0, s], atr.at[1, s], fw_s.at[k], fw_r.at[k], {"dp": sib})

    own_at.wait()
    forward(me, 0).start()

    @pl.loop(1, peers)
    def _(k):
        at_copy(k).wait_recv()
        forward(lax.rem(me - k + peers, peers), k).start()

    def g_copy(k):
        p = lax.rem(me + k, peers)
        return remote(g_ref.at[p], gr_ref.at[me], g_s.at[k], g_r.at[k], {"seq": p})

    @pl.loop(1, peers)
    def _(k):
        g_copy(k).start()

    @pl.loop(0, peers)
    def _(k):
        forward(lax.rem(me - k + peers, peers), k).wait_recv()

    dy_copy.wait_recv()
    own_dy.wait()

    way = tiles // 2

    def z_copy(t, step):
        up = 1 if t < way else -1
        chunk = lax.rem(zz - up * (1 + step) + 2 * nz, nz)
        return chunk, remote(
            part.at[t, chunk], ring.at[t, step], z_s.at[t, step], z_r.at[t, step], {"dp": at_z(up)}
        )

    order = [t + w for t in range(way) for w in (0, way)]
    for t in order:
        tc = slice(t * tcols, (t + 1) * tcols)

        @pl.loop(0, peers)
        def _(s):
            lhs = jnp.concatenate(
                [atr[q, s, b * feats : (b + 1) * feats, :] for q in range(2) for b in range(tb)], axis=1
            )
            rhs = jnp.concatenate([dyx[q, :, tc] for q in range(2)], axis=0)
            prod = lax.dot_general(lhs, rhs, NN, preferred_element_type=F32)
            for j in range(2):
                for z in range(nz):
                    r = (j * nz + z) * srows
                    part[t, z, s * 2 + j] = prod[r : r + srows].astype(BF16)

        z_copy(t, 0)[1].start()

    for step in range(nz - 1):
        for t in order:
            z_copy(t, step)[1].wait_recv()
            up = 1 if t < way else -1
            chunk = lax.rem(zz - up * (2 + step) + 2 * nz, nz)
            part[t, chunk] = (part[t, chunk].astype(F32) + ring[t, step].astype(F32)).astype(BF16)
            if step < nz - 2:
                z_copy(t, step + 1)[1].start()

    def p_copy(k):
        j, where = plane_peer(k)
        return remote(part.at[:, zz, j], plane.at[k], p_s.at[k], p_r.at[k], where)

    @pl.loop(1, slabs)
    def _(k):
        p_copy(k).start()

    total[...] = part[:, zz, my].astype(F32)

    @pl.loop(1, slabs)
    def _(k):
        p_copy(k).wait_recv()
        total[...] += plane[k].astype(F32)

    rows = gw_ref.shape[0]
    for c in range(2):
        half[c] = total[:, c * rows : (c + 1) * rows, :] * scale
    swap = remote(half.at[1 - core], other, o_s, o_r, {"dp": sib})
    swap.start()
    swap.wait_recv()
    for t in range(tiles):
        gw_ref[:, pl.ds(pl.multiple_of(core * cols + t * tcols, BLK), tcols)] = half[core, t]
        gw_ref[:, pl.ds(pl.multiple_of((1 - core) * cols + t * tcols, BLK), tcols)] = other[t]

    swap.wait_send()
    dy_copy.wait_send()
    own_g.wait()
    forward(me, 0).wait_send()

    @pl.loop(1, peers)
    def _(k):
        at_copy(k).wait_send()
        forward(lax.rem(me - k + peers, peers), k).wait_send()
        g_copy(k).wait()

    for step in range(nz - 1):
        for t in order:
            z_copy(t, step)[1].wait_send()

    @pl.loop(1, slabs)
    def _(k):
        p_copy(k).wait_send()


def bring_back(at, g, dy, scale):
    peers = at.shape[0]
    rows, depth = dy.shape
    tiles, tcols, nz, slabs = 6, 256, 4, 16
    out_rows = peers * 192 // 128
    dma = pltpu.SemaphoreType.DMA
    return pl.pallas_call(
        functools.partial(back_kernel, scale),
        out_shape=(jax.ShapeDtypeStruct(g.shape, BF16), jax.ShapeDtypeStruct((out_rows, depth), F32)),
        in_specs=[V, V, V],
        out_specs=(V, V),
        scratch_shapes=[
            pltpu.VMEM((2, *at.shape), BF16),
            pltpu.VMEM((2, rows, depth // 2), BF16),
            pltpu.VMEM((tiles, nz, slabs, 2 * out_rows, tcols), BF16),
            pltpu.VMEM((tiles, nz - 1, slabs, 2 * out_rows, tcols), BF16),
            pltpu.VMEM((slabs, tiles, 2 * out_rows, tcols), BF16),
            pltpu.VMEM((tiles, 2 * out_rows, tcols), F32),
            pltpu.VMEM((2, tiles, out_rows, tcols), F32),
            pltpu.VMEM((tiles, out_rows, tcols), F32),
            dma((peers,)), dma((peers,)), dma((peers,)), dma((peers,)), dma, dma,
            dma((peers,)), dma((peers,)), dma((tiles, nz - 1)), dma((tiles, nz - 1)),
            dma((slabs,)), dma((slabs,)), dma, dma, dma((3,)),
        ],
        compiler_params=pltpu.CompilerParams(
            collective_id=1, has_side_effects=True, vmem_limit_bytes=56 * 2**20
        ),
        cost_estimate=cost(2 * rows * depth * peers * 192, at, g, g, dy),
        name="bring_back",
    )(at, g, dy)


V = pl.BlockSpec(memory_space=pltpu.VMEM)
S = pl.BlockSpec(memory_space=pltpu.SMEM)


def cost(flops, *arrays):
    return pl.CostEstimate(
        flops=flops, bytes_accessed=sum(a.size * a.dtype.itemsize for a in arrays), transcendentals=0
    )


def attention(idx, cnt, x, d):
    heads, blocks = cnt.shape
    seq = blocks * BLK
    return pl.pallas_call(
        attn_kernel,
        out_shape=(jax.ShapeDtypeStruct(d.shape, BF16), jax.ShapeDtypeStruct(x.shape, BF16)),
        in_specs=[S, S, V, V],
        out_specs=(V, V),
        scratch_shapes=[
            pltpu.VMEM((heads, BLK, seq), BF16),
            pltpu.VMEM((heads, seq, BLK), F32),
        ],
        compiler_params=pltpu.CompilerParams(vmem_limit_bytes=48 * 2**20),
        cost_estimate=cost(60_000_000_000, x, d, x, d),
        name="attention",
    )(idx, cnt, x, d)


def wide(rows, cols, pos=1):
    return pl.BlockSpec((rows, cols), (lambda t: (0, t)) if pos else (lambda t: (t, 0)))


def local(query, key_states, value_states, grad_out, w_out, block_index, block_count):
    rows, hd = query.shape[1:]
    depth = grad_out.shape[2]
    n_seq, n_dp = lax.axis_size("seq"), lax.axis_size("dp")
    per = hd // HDIM // n_seq
    tiles = n_seq // 2
    cols = hd // tiles
    x_rows = per * rows + TB * per * HDIM
    d_rows = TB * per * HDIM
    packed = jax.ShapeDtypeStruct((n_seq, x_rows, BLK), BF16)
    small = jax.ShapeDtypeStruct((n_seq, d_rows, BLK), BF16)
    pairs = pl.BlockSpec((2, x_rows, BLK), lambda t: (t, 0, 0))
    pairs_d = pl.BlockSpec((2, d_rows, BLK), lambda t: (t, 0, 0))
    flat = jax.ShapeDtypeStruct((rows, hd), BF16)
    big = pltpu.CompilerParams(vmem_limit_bytes=48 * 2**20)
    q, k, v, dy = query[0], key_states[0], value_states[0], grad_out[0]

    def swap(x):
        return lax.all_to_all(x, "seq", split_axis=0, concat_axis=0, tiled=True)

    w_all = lax.all_gather(w_out, "dp", axis=0, tiled=True)
    x = pl.pallas_call(
        pack_kernel, out_shape=packed, grid=(tiles,), in_specs=[wide(rows, cols)] * 3, out_specs=pairs,
        cost_estimate=cost(0, q, k, v, packed), name="pack",
    )(q, k, v)
    x = swap(x)
    d = pl.pallas_call(
        project_kernel, out_shape=small, grid=(tiles,),
        in_specs=[pl.BlockSpec((rows, depth), lambda t: (0, 0)), wide(cols, depth, 0)],
        out_specs=pairs_d, compiler_params=big,
        cost_estimate=cost(2 * rows * depth * hd, dy, w_all, small), name="project",
    )(dy, w_all)
    d = swap(d)
    first = lax.axis_index("seq") * per
    idx = lax.dynamic_slice_in_dim(block_index, first, per, 0)
    cnt = lax.dynamic_slice_in_dim(block_count, first, per, 0)
    at, g = attention(idx, cnt, x, d)
    scale = float(rows * n_seq * n_dp) ** (-0.5)
    gr, gw = bring_back(at, g, dy, scale)
    dq, dk, dv = pl.pallas_call(
        unpack_kernel, out_shape=(flat,) * 3, grid=(tiles,), in_specs=[pairs],
        out_specs=(wide(rows, cols),) * 3, cost_estimate=cost(0, q, k, v, packed), name="unpack",
    )(gr)
    return dq[None], dk[None], dv[None], gw


def solution(mesh):
    tok = P("dp", "seq", None)
    return jax.shard_map(
        local,
        mesh=mesh,
        in_specs=(tok, tok, tok, tok, P("dp", None), P(), P()),
        out_specs=(tok, tok, tok, P(("seq", "dp"), None)),
        check_vma=False,
    )
```

time: 471 us -> 323 us (0.69)
  waiting for transfers between devices: 259 us -> 99.3 us
  Pallas kernels: 96.4 us -> 188 us
  blocking collectives: 74.7 us -> 0 us
    reduce_scatter x2 -> x0, waiting for transfers between devices: 155 us -> none  [the longest x1 123 us: local(): lax.psum_scatter(gw.reshape(n_seq, hd // n_seq, depth), 'seq', scatter_di...]
    pallas_call x4, Pallas kernels: 92.1 us -> 183 us  [the longest x1 111 us: bring_back(): pl.pallas_call(functools.partial(back_kernel, scale), out_shape=(jax.Shap...]
    all_to_all x2 -> x0, blocking collectives: 74.7 us -> none  [swap(): return lax.all_to_all(x, 'seq', split_axis=0, concat_axis=0, tiled=True)]
    all_to_all x2, waiting for transfers between devices: 30.1 us -> 13.3 us  [swap(): return lax.all_to_all(x, 'seq', split_axis=0, concat_axis=0, tiled=True)]
    all_gather x1, waiting for transfers between devices: 72.9 us -> 85.4 us  [local(): w_all = lax.all_gather(w_out, 'dp', axis=0, tiled=True)]
  transfers between devices with their start and end apart: 5 -> 3, of which waited for: 4 -> 2; matrix products, arithmetic and copies ran while one was open for 0% -> 0% of each run, Pallas kernels for 4% -> 4%
where the time goes in v2:
time: 323 us; the launch traced here: 320 us
  Pallas kernels  188 us (58%)
  waiting for transfers between devices  99.3 us (31%)
  starting transfers between devices  14.6 us (5%)
  between operations  14.1 us (4%)
  local copies, waits for them, and re-layouts  4.23 us (1%)
    pallas_call x1, Pallas kernels, bring_back(): pl.pallas_call(functools.partial(back_kernel, scale), out_shape=(jax.Shap...  111 us
    all_gather x1, waiting for transfers between devices, local(): w_all = lax.all_gather(w_out, 'dp', axis=0, tiled=True)  85.4 us
    pallas_call x1, Pallas kernels, attention(): pl.pallas_call(attn_kernel, out_shape=(jax.ShapeDtypeStruct(d.shape, BF16...  59.3 us
    all_to_all x2, starting transfers between devices, swap(): return lax.all_to_all(x, 'seq', split_axis=0, concat_axis=0, tiled=True)  14.5 us
    all_to_all x2, waiting for transfers between devices, swap(): return lax.all_to_all(x, 'seq', split_axis=0, concat_axis=0, tiled=True)  13.3 us
    pallas_call x1, Pallas kernels, local(): pl.pallas_call(project_kernel, out_shape=small, grid=(tiles,), in_specs=[...  8.47 us
  transfers between devices with their start and end apart: 3, of which 2 were waited for; matrix products, arithmetic and copies ran while one was open for 0% of the time, Pallas kernels for 4%

profile of v2, /device:TPU:116, one launch (start us, length us, event | category | flops | bytes accessed | tf_op | source)
XLA Modules:
  0.0 320.3 jit_solution(6427184399848150248)
XLA Ops:
  7.2 0.0 copy-start
  7.2 0.0 all-gather.2.cloned.1.call-start
  7.2 0.7 all-gather.2.cloned.1.call-update
  7.9 4.9 %pack.1 = bf16[8,1728,128]{2,1,0:T(8,128)(2,1)} custom-call(bf16[384,1536]{1,0:T(8,128)(2,1)} %bitcast.9, bf16[384,1536]{1,0:T(8,128)(2,1)} %bitcast.10, bf16[384,1536]{1,0:T(8,128)(2,1)} %bitcast.11), custom_call_target="tpu_custom_call" | custom-call | bytes 7077888 | tf_op jit(solution)/shard_map/pack/pallas_call | solution.py:392
  12.8 0.0 copy-start.1
  12.8 7.3 %all-to-all-start = ((bf16[8,1728,128]{2,1,0:T(8,128)(2,1)}), bf16[8,1728,128]{2,1,0:T(8,128)(2,1)}, u32[]{:S(2)}, u32[]{:S(2)}) async-start(bf16[8,1728,128]{2,1,0:T(8,128)(2,1)} %pack.1), calls=%async_computation | async-start | bytes 7077888 | tf_op jit(solution)/shard_map/all_to_all | solution.py:389
  20.1 85.4 %all-gather.2.cloned.1.call-done.w_ref = bf16[1536,3072]{1,0:T(8,128)(2,1)} async-done(((bf16[96,3072]{1,0:T(8,128)(2,1)}), bf16[1536,3072]{1,0:T(8,128)(2,1)}) %all-gather.2.cloned.1.call-update) | async-done | bytes 9437200 | tf_op jit(solution)/shard_map/all_gather | solution.py:391
  105.5 0.0 copy-done.1
  105.5 8.5 %project.1 = bf16[8,576,128]{2,1,0:T(8,128)(2,1)} custom-call(bf16[384,3072]{1,0:T(8,128)(2,1)S(1)} %bitcast.8, bf16[1536,3072]{1,0:T(8,128)(2,1)} %all-gather.2.cloned.1.call-done.w_ref), custom_call_target="tpu_custom_call" | custom-call | flops 3623878656 | bytes 12976128 | tf_op jit(solution)/shard_map/project/pallas_call | solution.py:397
  114.0 0.0 all-to-all-done.x_ref
  114.0 7.2 %all-to-all-start.1 = ((bf16[8,576,128]{2,1,0:T(8,128)(2,1)}), bf16[8,576,128]{2,1,0:T(8,128)(2,1)S(1)}, u32[]{:S(2)}, u32[]{:S(2)}) async-start(bf16[8,576,128]{2,1,0:T(8,128)(2,1)} %project.1), calls=%async_computation.1 | async-start | bytes 2359296 | tf_op jit(solution)/shard_map/all_to_all | solution.py:389
  121.2 0.0 copy-done
  121.2 0.1 copy.12.idx_ref
  121.2 0.7 constant_dynamic-slice_fusion.cnt_ref
  122.0 13.3 %all-to-all-done.1.d_ref = bf16[8,576,128]{2,1,0:T(8,128)(2,1)S(1)} async-done(((bf16[8,576,128]{2,1,0:T(8,128)(2,1)}), bf16[8,576,128]{2,1,0:T(8,128)(2,1)S(1)}, u32[]{:S(2)}, u32[]{:S(2)}) %all-to-all-start.1) | async-done | bytes 1179680 | tf_op jit(solution)/shard_map/all_to_all | solution.py:389
  135.2 59.3 %attention.1 = (bf16[8,576,128]{2,1,0:T(8,128)(2,1)S(1)}, bf16[8,1728,128]{2,1,0:T(8,128)(2,1)S(1)}) custom-call(s32[3,24,8]{2,1,0:T(8,128)S(1)} %copy.12.idx_ref, s32[3,24]{1,0:T(4,128)S(1)} %constant_dynamic-slice_fusion.cnt_ref, bf16[8,1728,128]{2,1,0:T(8,128)(2,1)} %all-to-all-done.x_ref, bf16[8,576,128]{2,1,0:T(8,128)(2,1)S(1)} %all-to-all-done.1.d_ref), custom_call_target="tpu_custom_call" | custom-call | flops 60000002048 | bytes 9437184 | tf_op jit(solution)/shard_map/attention/pallas_call | solution.py:352
  194.5 0.0 copy-start.2
  194.5 1.7 copy-done.2
  196.3 1.0 copy-done.3
  197.3 110.8 %bring_back.1 = (bf16[8,1728,128]{2,1,0:T(8,128)(2,1)}, f32[12,3072]{1,0:T(8,128)}) custom-call(bf16[8,576,128]{2,1,0:T(8,128)(2,1)} %copy-done.3, bf16[8,1728,128]{2,1,0:T(8,128)(2,1)} %copy-done.2, bf16[384,3072]{1,0:T(8,128)(2,1)} %bitcast.7), custom_call_target="tpu_custom_call" | custom-call | flops 3623878656 | bytes 10616832 | tf_op jit(solution)/shard_map/bring_back/pallas_call | solution.py:313
  308.1 0.0 copy-start.4
  308.1 4.7 %unpack.1 = (bf16[384,1536]{1,0:T(8,128)(2,1)}, bf16[384,1536]{1,0:T(8,128)(2,1)}, bf16[384,1536]{1,0:T(8,128)(2,1)}) custom-call(bf16[8,1728,128]{2,1,0:T(8,128)(2,1)} %get-tuple-element.13.x_ref), custom_call_target="tpu_custom_call" | custom-call | bytes 7077888 | tf_op jit(solution)/shard_map/unpack/pallas_call | solution.py:410
  312.8 0.0 copy-done.4
  312.8 0.7 copy.14
  (2 shorter events, 0.0 us)
Async XLA Ops:
  7.2 114.0 %copy-start = (s32[24,24,8]{1,2,0:T(8,128)S(1)}, s32[24,24,8]{1,2,0:T(8,128)}, u32[]{:S(2)}) copy-start(s32[24,24,8]{1,2,0:T(8,128)} %param.12) | copy-start | bytes 55300
  7.2 98.3 %all-gather.2.cloned.1.call-start = ((), (), s32[]{:S(2)}) async-start(), calls=%async_computation.2 | async-start | bytes 10027008 | tf_op jit(solution)/shard_map/all_gather | solution.py:391
  12.8 92.7 %copy-start.1 = (bf16[1,384,3072]{2,1,0:T(8,128)(2,1)S(1)}, bf16[1,384,3072]{2,1,0:T(8,128)(2,1)}, u32[]{:S(2)}) copy-start(bf16[1,384,3072]{2,1,0:T(8,128)(2,1)} %param.10) | copy-start | bytes 7077892
  12.8 101.2 %all-to-all-start = ((bf16[8,1728,128]{2,1,0:T(8,128)(2,1)}), bf16[8,1728,128]{2,1,0:T(8,128)(2,1)}, u32[]{:S(2)}, u32[]{:S(2)}) async-start(bf16[8,1728,128]{2,1,0:T(8,128)(2,1)} %pack.1), calls=%async_computation | async-start | bytes 7077888 | tf_op jit(solution)/shard_map/all_to_all | solution.py:389
  114.0 21.3 %all-to-all-start.1 = ((bf16[8,576,128]{2,1,0:T(8,128)(2,1)}), bf16[8,576,128]{2,1,0:T(8,128)(2,1)S(1)}, u32[]{:S(2)}, u32[]{:S(2)}) async-start(bf16[8,576,128]{2,1,0:T(8,128)(2,1)} %project.1), calls=%async_computation.1 | async-start | bytes 2359296 | tf_op jit(solution)/shard_map/all_to_all | solution.py:389
  194.5 1.8 copy-start.2
  196.3 1.0 copy-start.3
  308.1 4.7 %copy-start.4 = (f32[12,3072]{1,0:T(8,128)S(1)}, f32[12,3072]{1,0:T(8,128)}, u32[]{:S(2)}) copy-start(f32[12,3072]{1,0:T(8,128)} %get-tuple-element.25) | copy-start | bytes 442372
Sparse Core Ops, SparseCore 0:
  9.7 95.7 all-gather.1

commit v3 on v2

--- a/solution.py
+++ b/solution.py
@@ -19,28 +19,192 @@
 Q_AT = 1152
 
 
-def pack_kernel(q_ref, k_ref, v_ref, out_ref):
+def front_kernel(q_ref, k_ref, v_ref, dy_ref, w_ref, xr_ref, dr_ref, xs, ds, wall,
+                 x_s, x_r, d_s, d_r, z_s, z_r, y_s, y_r, f_s, f_r, loc):
+    dp, me = lax.axis_index("dp"), lax.axis_index("seq")
+    core, zz, lo = dp % 2, (dp // 2) % 4, dp // 8
+    sib, mate = dp + 1 - 2 * core, dp + 8 - 16 * lo
+    peers, nz = xs.shape[0], wall.shape[2]
+    rows = q_ref.shape[0]
+    feats = q_ref.shape[1] // peers
+    part = wall.shape[3] // 2
+
+    def at_z(k):
+        return lo * 8 + lax.rem(zz + k + nz, nz) * 2 + core
+
+    bar = pltpu.get_barrier_semaphore()
+
+    def hello(where):
+        pl.semaphore_signal(bar, inc=1, device_id=where, device_id_type=MESH)
+
+    @pl.loop(1, peers)
+    def _(k):
+        hello({"seq": lax.rem(me + k, peers)})
+
+    for where in (sib, mate, at_z(1), at_z(-1)):
+        hello({"dp": where})
+    pl.semaphore_wait(bar, peers + 3)
+
+    def remote(src, dst, ssem, rsem, where):
+        return pltpu.make_async_remote_copy(
+            src_ref=src, dst_ref=dst, send_sem=ssem, recv_sem=rsem, device_id=where, device_id_type=MESH
+        )
+
+    def row(l):
+        return lo if l == 0 else 1 - lo
+
+    def cell(l, k, c=None):
+        return wall.at[core if c is None else c, row(l), lax.rem(zz - k + nz, nz)]
+
+    def source(l):
+        return w_ref if l == 0 else cell(l, 0)
+
+    def hop(l, up):
+        d = 0 if up == 1 else 1
+        return remote(source(l), cell(l, 0), z_s.at[l, d, 0], z_r.at[l, d, 0], {"dp": at_z(up)})
+
+    def hop_in(l, up):
+        d = 0 if up == 1 else 1
+        return remote(cell(l, up), cell(l, up), z_s.at[l, d, 0], z_r.at[l, d, 0], {"dp": at_z(up)})
+
+    def relay(l, up):
+        d = 0 if up == 1 else 1
+        h = pl.ds(d * part, part)
+        c = cell(l, up).at[h]
+        return remote(c, c, z_s.at[l, d, 1], z_r.at[l, d, 1], {"dp": at_z(up)})
+
+    def relay_in(l, up):
+        d = 0 if up == 1 else 1
+        h = pl.ds(d * part, part)
+        c = cell(l, 2).at[h]
+        return remote(c, c, z_s.at[l, d, 1], z_r.at[l, d, 1], {"dp": at_z(up)})
+
+    def over(l, k):
+        return remote(
+            w_ref if (l, k) == (0, 0) else cell(l, k), cell(l, k), f_s.at[l, k], f_r.at[l, k], {"dp": sib}
+        )
+
+    def over_in(l, k):
+        c = cell(l, k, 1 - core)
+        return remote(c, c, f_s.at[l, k], f_r.at[l, k], {"dp": sib})
+
+    hop(0, 1).start()
+    hop(0, -1).start()
+    to_mate = remote(w_ref, cell(0, 0), y_s, y_r, {"dp": mate})
+    to_mate.start()
+    over(0, 0).start()
+    own_w = pltpu.make_async_copy(w_ref, cell(0, 0), loc.at[0])
+    own_w.start()
+
     k, v = k_ref[...], v_ref[...]
-    rows = k.shape[0]
-    qt = q_ref[...].T
-    feats = qt.shape[0] // 2
-    for peer in range(2):
+    for p in range(peers):
         for j in range(feats // HDIM):
-            cols = slice(peer * feats + j * HDIM, peer * feats + (j + 1) * HDIM)
-            out_ref[peer, j * rows : (j + 1) * rows] = jnp.concatenate([k[:, cols], v[:, cols]], axis=1)
-        for t in range(rows // BLK):
-            at = Q_AT + t * feats
-            out_ref[peer, at : at + feats] = qt[peer * feats : (peer + 1) * feats, t * BLK : (t + 1) * BLK]
-
-
-def project_kernel(dy_ref, w_ref, out_ref):
-    d = lax.dot_general(w_ref[...], dy_ref[...], NT, preferred_element_type=F32).astype(BF16)
-    feats = d.shape[0] // 2
-    for peer in range(2):
-        for t in range(d.shape[1] // BLK):
-            out_ref[peer, t * feats : (t + 1) * feats] = d[
-                peer * feats : (peer + 1) * feats, t * BLK : (t + 1) * BLK
-            ]
+            cols = slice(p * feats + j * HDIM, p * feats + (j + 1) * HDIM)
+            xs[p, j * rows : (j + 1) * rows] = jnp.concatenate([k[:, cols], v[:, cols]], axis=1)
+    for p in range(0, peers, 2):
+        qt = q_ref[:, p * feats : (p + 2) * feats].T
+        for i in range(2):
+            for t in range(TB):
+                at = Q_AT + t * feats
+                xs[p + i, at : at + feats] = qt[i * feats : (i + 1) * feats, t * BLK : (t + 1) * BLK]
+
+    def x_copy(k):
+        p = lax.rem(me + k, peers)
+        return remote(xs.at[p], xr_ref.at[me], x_s.at[k], x_r.at[k], {"seq": p})
+
+    @pl.loop(1, peers)
+    def _(k):
+        x_copy(k).start()
+
+    own_x = pltpu.make_async_copy(xs.at[me], xr_ref.at[me], loc.at[1])
+    own_x.start()
+    own_w.wait()
+
+    def d_copy(n, s):
+        return remote(ds.at[s], dr_ref.at[me], d_s.at[n], d_r.at[me], {"seq": s})
+
+    def own_d():
+        return pltpu.make_async_copy(ds.at[me], dr_ref.at[me], loc.at[2])
+
+    def peer(l, k):
+        return row(l) * nz + lax.rem(zz - k + nz, nz)
+
+    def project(n, l, k):
+        over_in(l, k).wait_recv()
+        s, z = peer(l, k), lax.rem(zz - k + nz, nz)
+        w2 = jnp.concatenate([wall[0, row(l), z], wall[1, row(l), z]], axis=0)
+        d = lax.dot_general(w2, dy_ref[...], NT, preferred_element_type=F32).astype(BF16)
+        for t in range(TB):
+            ds[s, t * feats : (t + 1) * feats] = d[:, t * BLK : (t + 1) * BLK]
+
+        @pl.when(s != me)
+        def _():
+            d_copy(n, s).start()
+
+        @pl.when(s == me)
+        def _():
+            own_d().start()
+
+    order = [(0, 0), (1, 0), (0, 1), (0, 3), (1, 1), (1, 3), (0, 2), (1, 2)]
+
+    def spread(l):
+        hop_in(l, 1).wait_recv()
+        relay(l, 1).start()
+        over(l, 1).start()
+        hop_in(l, -1).wait_recv()
+        relay(l, -1).start()
+        over(l, 3).start()
+
+    def finish(l):
+        relay_in(l, 1).wait_recv()
+        relay_in(l, -1).wait_recv()
+        over(l, 2).start()
+
+    project(0, *order[0])
+    remote(cell(1, 0), cell(1, 0), y_s, y_r, {"dp": mate}).wait_recv()
+    hop(1, 1).start()
+    hop(1, -1).start()
+    over(1, 0).start()
+    spread(0)
+    project(1, *order[1])
+    project(2, *order[2])
+    project(3, *order[3])
+    spread(1)
+    project(4, *order[4])
+    project(5, *order[5])
+    finish(0)
+    project(6, *order[6])
+    finish(1)
+    project(7, *order[7])
+
+    for l in range(2):
+        for up in (1, -1):
+            hop(l, up).wait_send()
+            relay(l, up).wait_send()
+        for k in range(nz):
+            over(l, k).wait_send()
+    to_mate.wait_send()
+    own_x.wait()
+
+    @pl.loop(1, peers)
+    def _(k):
+        x_copy(k).wait()
+
+    for n, (l, k) in enumerate(order):
+        s = peer(l, k)
+
+        @pl.when(s != me)
+        def _():
+            d_copy(n, s).wait_send()
+
+        @pl.when(s == me)
+        def _():
+            own_d().wait()
+
+    @pl.loop(1, peers)
+    def _(k):
+        p = lax.rem(me + k, peers)
+        remote(ds.at[p], dr_ref.at[p], d_s.at[0], d_r.at[p], {"seq": p}).wait_recv()
 
 
 def unpack_kernel(x_ref, q_ref, k_ref, v_ref):
@@ -364,8 +528,8 @@
     )(idx, cnt, x, d)
 
 
-def wide(rows, cols, pos=1):
-    return pl.BlockSpec((rows, cols), (lambda t: (0, t)) if pos else (lambda t: (t, 0)))
+def wide(rows, cols):
+    return pl.BlockSpec((rows, cols), lambda t: (0, t))
 
 
 def local(query, key_states, value_states, grad_out, w_out, block_index, block_count):
@@ -380,27 +544,28 @@
     packed = jax.ShapeDtypeStruct((n_seq, x_rows, BLK), BF16)
     small = jax.ShapeDtypeStruct((n_seq, d_rows, BLK), BF16)
     pairs = pl.BlockSpec((2, x_rows, BLK), lambda t: (t, 0, 0))
-    pairs_d = pl.BlockSpec((2, d_rows, BLK), lambda t: (t, 0, 0))
     flat = jax.ShapeDtypeStruct((rows, hd), BF16)
-    big = pltpu.CompilerParams(vmem_limit_bytes=48 * 2**20)
     q, k, v, dy = query[0], key_states[0], value_states[0], grad_out[0]
 
-    def swap(x):
-        return lax.all_to_all(x, "seq", split_axis=0, concat_axis=0, tiled=True)
-
-    w_all = lax.all_gather(w_out, "dp", axis=0, tiled=True)
-    x = pl.pallas_call(
-        pack_kernel, out_shape=packed, grid=(tiles,), in_specs=[wide(rows, cols)] * 3, out_specs=pairs,
-        cost_estimate=cost(0, q, k, v, packed), name="pack",
-    )(q, k, v)
-    x = swap(x)
-    d = pl.pallas_call(
-        project_kernel, out_shape=small, grid=(tiles,),
-        in_specs=[pl.BlockSpec((rows, depth), lambda t: (0, 0)), wide(cols, depth, 0)],
-        out_specs=pairs_d, compiler_params=big,
-        cost_estimate=cost(2 * rows * depth * hd, dy, w_all, small), name="project",
-    )(dy, w_all)
-    d = swap(d)
+    dma = pltpu.SemaphoreType.DMA
+    x, d = pl.pallas_call(
+        front_kernel,
+        out_shape=(packed, small),
+        in_specs=[V] * 5,
+        out_specs=(V, V),
+        scratch_shapes=[
+            pltpu.VMEM(packed.shape, BF16),
+            pltpu.VMEM(small.shape, BF16),
+            pltpu.VMEM((2, 2, n_dp // 4, *w_out.shape), BF16),
+            dma((n_seq,)), dma((n_seq,)), dma((n_seq,)), dma((n_seq,)),
+            dma((2, 2, 2)), dma((2, 2, 2)), dma, dma, dma((2, 4)), dma((2, 4)), dma((3,)),
+        ],
+        compiler_params=pltpu.CompilerParams(
+            collective_id=0, has_side_effects=True, vmem_limit_bytes=56 * 2**20
+        ),
+        cost_estimate=cost(2 * rows * depth * hd, q, k, v, dy, packed),
+        name="front",
+    )(q, k, v, dy, w_out)
     first = lax.axis_index("seq") * per
     idx = lax.dynamic_slice_in_dim(block_index, first, per, 0)
     cnt = lax.dynamic_slice_in_dim(block_count, first, per, 0)

time: 323 us -> 274 us (0.85)
  waiting for transfers between devices: 99.3 us -> 0 us
  Pallas kernels: 188 us -> 262 us
  starting transfers between devices: 14.6 us -> 0 us
  between operations: 14.1 us -> 0.7 us
    all_gather x1 -> x0, waiting for transfers between devices: 85.4 us -> none  [local(): w_all = lax.all_gather(w_out, 'dp', axis=0, tiled=True)]
    pallas_call x2 -> x1, Pallas kernels: 13.3 us -> 88.2 us  [local(): pl.pallas_call(front_kernel, out_shape=(packed, small), in_specs=[V] * 5,...]
    all_to_all x2 -> x0, starting transfers between devices: 14.5 us -> none  [swap(): return lax.all_to_all(x, 'seq', split_axis=0, concat_axis=0, tiled=True)]
    all_to_all x2 -> x0, waiting for transfers between devices: 13.3 us -> none  [swap(): return lax.all_to_all(x, 'seq', split_axis=0, concat_axis=0, tiled=True)]
    pallas_call x1, Pallas kernels: 111 us -> 101 us  [bring_back(): pl.pallas_call(functools.partial(back_kernel, scale), out_shape=(jax.Shap...]
    pallas_call x1, Pallas kernels: 59.3 us -> 68.8 us  [attention(): pl.pallas_call(attn_kernel, out_shape=(jax.ShapeDtypeStruct(d.shape, BF16...]
  transfers between devices with their start and end apart: 3 -> 0, of which waited for: 2 -> 0; matrix products, arithmetic and copies ran while one was open for 0% -> 0% of each run, Pallas kernels for 4% -> 0%
where the time goes in v3:
time: 274 us; the launch traced here: 269 us
  Pallas kernels  262 us (96%)
  local copies, waits for them, and re-layouts  5.67 us (2%)
    pallas_call x1, Pallas kernels, bring_back(): pl.pallas_call(functools.partial(back_kernel, scale), out_shape=(jax.Shap...  101 us
    pallas_call x1, Pallas kernels, local(): pl.pallas_call(front_kernel, out_shape=(packed, small), in_specs=[V] * 5,...  88.2 us
    pallas_call x1, Pallas kernels, attention(): pl.pallas_call(attn_kernel, out_shape=(jax.ShapeDtypeStruct(d.shape, BF16...  68.8 us

profile of v3, /device:TPU:116, one launch (start us, length us, event | category | flops | bytes accessed | tf_op | source)
XLA Modules:
  0.0 268.8 jit_solution(16473637500386839793)
XLA Ops:
  0.6 0.0 copy-start
  0.7 0.7 constant_dynamic-slice_fusion.cnt_ref
  1.4 0.1 copy-done
  1.5 0.1 copy.12.idx_ref
  1.6 88.2 %front.1 = (bf16[8,1728,128]{2,1,0:T(8,128)(2,1)}, bf16[8,576,128]{2,1,0:T(8,128)(2,1)}) custom-call(bf16[384,1536]{1,0:T(8,128)(2,1)} %bitcast.9, bf16[384,1536]{1,0:T(8,128)(2,1)} %bitcast.10, bf16[384,1536]{1,0:T(8,128)(2,1)} %bitcast.11, bf16[384,3072]{1,0:T(8,128)(2,1)} %bitcast.7, bf16[96,3072]{1,0:T(8,128)(2,1)} %w_ref.1), custom_call_target="tpu_custom_call" | custom-call | flops 3623878656 | bytes 9437184 | tf_op jit(solution)/shard_map/front/pallas_call | solution.py:551
  89.9 0.0 copy-start.3
  89.9 1.3 copy-done.3
  91.1 68.8 %attention.1 = (bf16[8,576,128]{2,1,0:T(8,128)(2,1)S(1)}, bf16[8,1728,128]{2,1,0:T(8,128)(2,1)S(1)}) custom-call(s32[3,24,8]{2,1,0:T(8,128)S(1)} %copy.12.idx_ref, s32[3,24]{1,0:T(4,128)S(1)} %constant_dynamic-slice_fusion.cnt_ref, bf16[8,1728,128]{2,1,0:T(8,128)(2,1)} %get-tuple-element.13.x_ref, bf16[8,576,128]{2,1,0:T(8,128)(2,1)S(1)} %copy-done.3), custom_call_target="tpu_custom_call" | custom-call | flops 60000002048 | bytes 9437184 | tf_op jit(solution)/shard_map/attention/pallas_call | solution.py:516
  160.0 0.0 copy-start.1
  160.0 1.7 copy-done.1
  161.7 0.0 copy-start.2
  161.7 1.0 copy-done.2
  162.7 100.6 %bring_back.1 = (bf16[8,1728,128]{2,1,0:T(8,128)(2,1)}, f32[12,3072]{1,0:T(8,128)}) custom-call(bf16[8,576,128]{2,1,0:T(8,128)(2,1)} %copy-done.2, bf16[8,1728,128]{2,1,0:T(8,128)(2,1)} %copy-done.1, bf16[384,3072]{1,0:T(8,128)(2,1)} %bitcast.8), custom_call_target="tpu_custom_call" | custom-call | flops 3623878656 | bytes 10616832 | tf_op jit(solution)/shard_map/bring_back/pallas_call | solution.py:477
  263.4 0.0 copy-start.4
  263.4 4.7 %unpack.1 = (bf16[384,1536]{1,0:T(8,128)(2,1)}, bf16[384,1536]{1,0:T(8,128)(2,1)}, bf16[384,1536]{1,0:T(8,128)(2,1)}) custom-call(bf16[8,1728,128]{2,1,0:T(8,128)(2,1)} %get-tuple-element.17.x_ref), custom_call_target="tpu_custom_call" | custom-call | bytes 7077888 | tf_op jit(solution)/shard_map/unpack/pallas_call | solution.py:575
  268.1 0.0 copy-done.4
  268.1 0.7 copy.14
  (1 shorter events, 0.0 us)
Async XLA Ops:
  0.6 0.9 copy-start
  89.9 1.3 copy-start.3
  160.0 1.8 copy-start.1
  161.7 1.0 copy-start.2
  263.4 4.7 %copy-start.4 = (f32[12,3072]{1,0:T(8,128)S(1)}, f32[12,3072]{1,0:T(8,128)}, u32[]{:S(2)}) copy-start(f32[12,3072]{1,0:T(8,128)} %get-tuple-element.29) | copy-start | bytes 442372

commit v4 on v3

--- a/solution.py
+++ b/solution.py
@@ -15,6 +15,7 @@
 BF16 = jnp.bfloat16
 F32 = jnp.float32
 MESH = pl.DeviceIdType.MESH
+REACH = 4
 TB = 3
 Q_AT = 1152
 
@@ -226,86 +227,60 @@
     v_ref[...] = jnp.concatenate(vs, axis=1)
 
 
-def attn_block(n, h, i, idx_ref, x_ref, d_ref, kvt_ref, acc_ref, at_ref, g_ref):
-    tb = TB
-    feats = d_ref.shape[1] // tb
-    per = tb * BLK
-
-    def key_rows(b):
-        return pl.ds(pl.multiple_of(h * per + (b % tb) * BLK, BLK), BLK)
-
+def attend(jobs, bias_ref, x_ref, d_ref, kvt_ref, acc_ref, at_ref, g_ref):
+    feats = d_ref.shape[1] // TB
+    per = TB * BLK
+    blocks = x_ref.shape[0] * TB
+    width = 2 * REACH + 1
     def seq_rows(b):
         return pl.ds(pl.multiple_of(b * BLK, BLK), BLK)
-
-    at = pl.multiple_of((i % tb) * feats + h * HDIM, HDIM)
-    qt = x_ref[i // tb, pl.ds(pl.multiple_of(Q_AT + at, HDIM), HDIM), :] * BF16(HDIM**-0.5)
-    dt = d_ref[i // tb, pl.ds(at, HDIM), :]
-    zero = jnp.zeros_like(qt)
-    both = jnp.concatenate(
-        [jnp.concatenate([qt, zero], axis=1), jnp.concatenate([zero, dt], axis=1)], axis=0
-    )
-    ids = [idx_ref[h, i, m] for m in range(n)]
-    sd = [
-        lax.dot_general(x_ref[b // tb, key_rows(b), :], both, NN, preferred_element_type=F32)
-        for b in ids
-    ]
-    s = [x[:, :BLK] for x in sd]
-    dp = [x[:, BLK:] for x in sd]
-    top = jnp.max(functools.reduce(jnp.maximum, s), axis=0, keepdims=True)
-    w = [jnp.exp(x - top) for x in s]
-    inv = 1.0 / jnp.sum(functools.reduce(jnp.add, w), axis=0, keepdims=True)
-    p = [x * inv for x in w]
-    delta = jnp.sum(
-        functools.reduce(jnp.add, [a * b for a, b in zip(p, dp)]), axis=0, keepdims=True
-    )
-    ds = [a * (b - delta) for a, b in zip(p, dp)]
-    dsp = [jnp.concatenate([a.astype(BF16), b.astype(BF16)], axis=1) for a, b in zip(ds, p)]
-    for m in range(n):
-        acc_ref[h, seq_rows(ids[m]), :] += lax.dot_general(
-            dsp[m], both, NT, preferred_element_type=F32
-        )
-    kt = jnp.concatenate([kvt_ref[h, :, seq_rows(b)] for b in ids], axis=1)
-    o = lax.dot_general(kt, jnp.concatenate(dsp, axis=0), NN, preferred_element_type=F32)
-    g_ref[i // tb, pl.ds(pl.multiple_of(Q_AT + at, HDIM), HDIM), :] = (
-        o[:HDIM, :BLK] * HDIM**-0.5
-    ).astype(BF16)
-    at_ref[i // tb, pl.ds(at, HDIM), :] = o[HDIM:, BLK:].astype(BF16)
-
-
-def attn_kernel(idx_ref, cnt_ref, x_ref, d_ref, at_ref, g_ref, kvt_ref, acc_ref):
-    heads, blocks = cnt_ref.shape
-    tb = blocks // x_ref.shape[0]
-    slots = idx_ref.shape[2]
-
-    def key_rows(h, b):
-        return pl.ds(pl.multiple_of(h * tb * BLK + (b % tb) * BLK, BLK), BLK)
-
-    def seq_rows(b):
-        return pl.ds(pl.multiple_of(b * BLK, BLK), BLK)
-
-    @pl.loop(0, heads)
-    def _(h):
-        @pl.loop(0, blocks)
-        def _(j):
-            kvt_ref[h, :, seq_rows(j)] = x_ref[j // tb, key_rows(h, j), :].T
-            acc_ref[h, seq_rows(j), :] = jnp.zeros((BLK, BLK), F32)
-
-        @pl.loop(0, blocks)
-        def _(i):
-            c = cnt_ref[h, i]
-            for n in range(1, slots + 1):
-
-                @pl.when(c == n)
-                def _():
-                    attn_block(n, h, i, idx_ref, x_ref, d_ref, kvt_ref, acc_ref, at_ref, g_ref)
-
-        @pl.loop(0, blocks)
-        def _(j):
-            g_ref[j // tb, key_rows(h, j), :] = acc_ref[h, seq_rows(j), :].astype(BF16)
-
-
-def back_kernel(scale, at_ref, g_ref, dy_ref, gr_ref, gw_ref, atr, dyx, part, ring, plane, total, half, other,
-                at_s, at_r, fw_s, fw_r, dy_s, dy_r, g_s, g_r, z_s, z_r, p_s, p_r, o_s, o_r, loc):
+    st = []
+    for h, i in jobs:
+        at = (i % TB) * feats + h * HDIM
+        here = pl.ds(pl.multiple_of(at, HDIM), HDIM)
+        there = pl.ds(pl.multiple_of(Q_AT + at, HDIM), HDIM)
+        qt = x_ref[i // TB, there, :] * BF16(HDIM**-0.5)
+        dt = d_ref[i // TB, here, :]
+        zero = jnp.zeros_like(qt)
+        both = jnp.concatenate([jnp.concatenate([qt, zero], axis=1), jnp.concatenate([zero, dt], axis=1)], axis=0)
+        ids = [lax.rem(i + o + blocks - REACH, blocks) for o in range(width)]
+        sd = [lax.dot_general(x_ref[b // TB, pl.ds(pl.multiple_of(h * per + (b % TB) * BLK, BLK), BLK), :], both, NN, preferred_element_type=F32) for b in ids]
+        st.append((h, i, here, there, qt, dt, ids, sd))
+    outs = []
+    for h, i, here, there, qt, dt, ids, sd in st:
+        s = [sd[o][:, :BLK] + bias_ref[(h * blocks + i) * width + o] if o != REACH else sd[o][:, :BLK] for o in range(width)]
+        dp = [a[:, BLK:] for a in sd]
+        top = jnp.max(functools.reduce(jnp.maximum, s), axis=0, keepdims=True)
+        w = [jnp.exp(a - top) for a in s]
+        inv = 1.0 / jnp.sum(functools.reduce(jnp.add, w), axis=0, keepdims=True)
+        delta = jnp.sum(functools.reduce(jnp.add, [a * b for a, b in zip(w, dp)]), axis=0, keepdims=True) * inv
+        ds = [a * (b - delta) for a, b in zip(w, dp)]
+        dsp = [jnp.concatenate([a.astype(BF16), b.astype(BF16)], axis=1) for a, b in zip(ds, w)]
+        qi = (qt.astype(F32) * inv).astype(BF16)
+        di = (dt.astype(F32) * inv).astype(BF16)
+        zero = jnp.zeros_like(qi)
+        both = jnp.concatenate([jnp.concatenate([qi, zero], axis=1), jnp.concatenate([zero, di], axis=1)], axis=0)
+        gr = [lax.dot_general(a, both, NT, preferred_element_type=F32) for a in dsp]
+        kt = jnp.concatenate([kvt_ref[h, :, seq_rows(b)] for b in ids], axis=1)
+        o = lax.dot_general(kt, jnp.concatenate(dsp, axis=0), NN, preferred_element_type=F32)
+        outs.append((gr, o, inv))
+    for (h, i, here, there, qt, dt, ids, sd), (gr, o, inv) in zip(st, outs):
+        for b, a in zip(ids, gr):
+            acc_ref[h, seq_rows(b), :] += a
+        g_ref[i // TB, there, :] = (o[:HDIM, :BLK] * (inv * HDIM**-0.5)).astype(BF16)
+        at_ref[i // TB, here, :] = (o[HDIM:, BLK:] * inv).astype(BF16)
+
+
+def make_bias(idx, cnt):
+    heads, blocks, slots = idx.shape
+    rel = (idx - jnp.arange(blocks)[None, :, None] + REACH) % blocks
+    live = jnp.arange(slots) < cnt[:, :, None]
+    hit = jnp.any((rel[..., None] == jnp.arange(2 * REACH + 1)) & live[..., None], axis=2)
+    return jnp.where(hit, 0.0, -1e30).astype(F32).reshape(-1)
+
+
+def rest_kernel(scale, bias_ref, x_ref, d_ref, dy_ref, gr_ref, gw_ref, at_ref, g_ref, kvt, acc, atr, dyx, part, ring, plane, total, half, other,
+                at_s, at_r, fw_s, fw_r, dy_s, dy_r, q_s, q_r, g_s, g_r, z_s, z_r, p_s, p_r, o_s, o_r, loc):
     dp, me = lax.axis_index("dp"), lax.axis_index("seq")
     core, zz, lo = dp % 2, (dp // 2) % 4, dp // 8
     sib = dp + 1 - 2 * core
@@ -346,38 +321,90 @@
         p = lax.rem(me + k, peers)
         return remote(at_ref.at[p], atr.at[0, me], at_s.at[k], at_r.at[k], {"seq": p})
 
-    @pl.loop(1, peers)
-    def _(k):
-        at_copy(k).start()
-
     mine = pl.ds(pl.multiple_of(core * cols, BLK), cols)
     theirs = pl.ds(pl.multiple_of((1 - core) * cols, BLK), cols)
     dy_copy = remote(dy_ref.at[:, theirs], dyx.at[1], dy_s, dy_r, {"dp": sib})
     dy_copy.start()
     own_dy = pltpu.make_async_copy(dy_ref.at[:, mine], dyx.at[0], loc.at[0])
     own_dy.start()
+
+    heads = acc.shape[0]
+
+    def q_copy(k):
+        p = lax.rem(me + k, peers)
+        r = pl.ds(Q_AT, feats * tb)
+        return remote(g_ref.at[p, r], gr_ref.at[me, r], q_s.at[k], q_r.at[k], {"seq": p})
+
+    def g_copy(k):
+        p = lax.rem(me + k, peers)
+        r = pl.ds(0, Q_AT)
+        return remote(g_ref.at[p, r], gr_ref.at[me, r], g_s.at[k], g_r.at[k], {"seq": p})
+
+    def forward(s, k):
+        return remote(atr.at[0, s], atr.at[1, s], fw_s.at[k], fw_r.at[k], {"dp": sib})
+
+    def arrived(k):
+        at_copy(k).wait_recv()
+        forward(lax.rem(me - k + peers, peers), k).start()
+
+    def key_rows(h, t):
+        return pl.ds(pl.multiple_of((h * tb + t) * BLK, BLK), BLK)
+
+    def seq_rows(b):
+        return pl.ds(pl.multiple_of(b * BLK, BLK), BLK)
+
+    @pl.loop(0, peers * tb)
+    def _(j):
+        for h in range(heads):
+            kvt[h, :, seq_rows(j)] = x_ref[j // tb, key_rows(h, lax.rem(j, tb)), :].T
+            acc[h, seq_rows(j), :] = jnp.zeros((BLK, BLK), F32)
+
+    def settle(k):
+        c = lax.rem(me + k, peers)
+        for h in range(heads):
+            for t in range(tb):
+                g_ref[c, key_rows(h, t), :] = acc[h, seq_rows(c * tb + t), :].astype(BF16)
+
+    @pl.loop(0, peers // 2)
+    def _(pair):
+        @pl.loop(0, tb)
+        def _(u):
+            b0 = (me + 1 + 2 * pair) * tb + 2 * u
+            attend(
+                [(h, lax.rem(b0 + t, peers * tb)) for t in range(2) for h in range(heads)],
+                bias_ref, x_ref, d_ref, kvt, acc, at_ref, g_ref,
+            )
+
+        at_copy(2 * pair + 1).start()
+        q_copy(2 * pair + 1).start()
+
+        @pl.when(pair < peers // 2 - 1)
+        def _():
+            at_copy(2 * pair + 2).start()
+            q_copy(2 * pair + 2).start()
+
+        @pl.when(pair > 0)
+        def _():
+            arrived(2 * pair - 1)
+            arrived(2 * pair)
+
+        @pl.when(pair == peers // 2 - 2)
+        def _():
+            for k in (3, 4):
+                settle(k)
+                g_copy(k).start()
+
     own_at = pltpu.make_async_copy(at_ref.at[me], atr.at[0, me], loc.at[1])
     own_at.start()
+    late = (1, 2, *range(5, peers))
+    for k in (*late, 0):
+        settle(k)
     own_g = pltpu.make_async_copy(g_ref.at[me], gr_ref.at[me], loc.at[2])
     own_g.start()
-
-    def forward(s, k):
-        return remote(atr.at[0, s], atr.at[1, s], fw_s.at[k], fw_r.at[k], {"dp": sib})
-
     own_at.wait()
     forward(me, 0).start()
-
-    @pl.loop(1, peers)
-    def _(k):
-        at_copy(k).wait_recv()
-        forward(lax.rem(me - k + peers, peers), k).start()
-
-    def g_copy(k):
-        p = lax.rem(me + k, peers)
-        return remote(g_ref.at[p], gr_ref.at[me], g_s.at[k], g_r.at[k], {"seq": p})
-
-    @pl.loop(1, peers)
-    def _(k):
+    arrived(peers - 1)
+    for k in late:
         g_copy(k).start()
 
     @pl.loop(0, peers)
@@ -457,6 +484,7 @@
     def _(k):
         at_copy(k).wait_send()
         forward(lax.rem(me - k + peers, peers), k).wait_send()
+        q_copy(k).wait()
         g_copy(k).wait()
 
     for step in range(nz - 1):
@@ -468,19 +496,25 @@
         p_copy(k).wait_send()
 
 
-def bring_back(at, g, dy, scale):
-    peers = at.shape[0]
+def rest(bias, x, d, dy, scale):
+    peers = x.shape[0]
     rows, depth = dy.shape
     tiles, tcols, nz, slabs = 6, 256, 4, 16
-    out_rows = peers * 192 // 128
+    feats = d.shape[1] // TB
+    heads, seq = feats // HDIM, peers * TB * BLK
+    out_rows = peers * feats // 128
     dma = pltpu.SemaphoreType.DMA
     return pl.pallas_call(
-        functools.partial(back_kernel, scale),
-        out_shape=(jax.ShapeDtypeStruct(g.shape, BF16), jax.ShapeDtypeStruct((out_rows, depth), F32)),
-        in_specs=[V, V, V],
+        functools.partial(rest_kernel, scale),
+        out_shape=(jax.ShapeDtypeStruct(x.shape, BF16), jax.ShapeDtypeStruct((out_rows, depth), F32)),
+        in_specs=[S, V, V, V],
         out_specs=(V, V),
         scratch_shapes=[
-            pltpu.VMEM((2, *at.shape), BF16),
+            pltpu.VMEM(d.shape, BF16),
+            pltpu.VMEM(x.shape, BF16),
+            pltpu.VMEM((heads, BLK, seq), BF16),
+            pltpu.VMEM((heads, seq, BLK), F32),
+            pltpu.VMEM((2, *d.shape), BF16),
             pltpu.VMEM((2, rows, depth // 2), BF16),
             pltpu.VMEM((tiles, nz, slabs, 2 * out_rows, tcols), BF16),
             pltpu.VMEM((tiles, nz - 1, slabs, 2 * out_rows, tcols), BF16),
@@ -489,15 +523,16 @@
             pltpu.VMEM((2, tiles, out_rows, tcols), F32),
             pltpu.VMEM((tiles, out_rows, tcols), F32),
             dma((peers,)), dma((peers,)), dma((peers,)), dma((peers,)), dma, dma,
-            dma((peers,)), dma((peers,)), dma((tiles, nz - 1)), dma((tiles, nz - 1)),
+            dma((peers,)), dma((peers,)), dma((peers,)), dma((peers,)),
+            dma((tiles, nz - 1)), dma((tiles, nz - 1)),
             dma((slabs,)), dma((slabs,)), dma, dma, dma((3,)),
         ],
         compiler_params=pltpu.CompilerParams(
-            collective_id=1, has_side_effects=True, vmem_limit_bytes=56 * 2**20
+            collective_id=1, has_side_effects=True, vmem_limit_bytes=60 * 2**20
         ),
-        cost_estimate=cost(2 * rows * depth * peers * 192, at, g, g, dy),
-        name="bring_back",
-    )(at, g, dy)
+        cost_estimate=cost(2 * rows * depth * peers * feats, x, d, x, dy),
+        name="rest",
+    )(bias, x, d, dy)
 
 
 V = pl.BlockSpec(memory_space=pltpu.VMEM)
@@ -508,24 +543,6 @@
     return pl.CostEstimate(
         flops=flops, bytes_accessed=sum(a.size * a.dtype.itemsize for a in arrays), transcendentals=0
     )
-
-
-def attention(idx, cnt, x, d):
-    heads, blocks = cnt.shape
-    seq = blocks * BLK
-    return pl.pallas_call(
-        attn_kernel,
-        out_shape=(jax.ShapeDtypeStruct(d.shape, BF16), jax.ShapeDtypeStruct(x.shape, BF16)),
-        in_specs=[S, S, V, V],
-        out_specs=(V, V),
-        scratch_shapes=[
-            pltpu.VMEM((heads, BLK, seq), BF16),
-            pltpu.VMEM((heads, seq, BLK), F32),
-        ],
-        compiler_params=pltpu.CompilerParams(vmem_limit_bytes=48 * 2**20),
-        cost_estimate=cost(60_000_000_000, x, d, x, d),
-        name="attention",
-    )(idx, cnt, x, d)
 
 
 def wide(rows, cols):
@@ -569,9 +586,8 @@
     first = lax.axis_index("seq") * per
     idx = lax.dynamic_slice_in_dim(block_index, first, per, 0)
     cnt = lax.dynamic_slice_in_dim(block_count, first, per, 0)
-    at, g = attention(idx, cnt, x, d)
     scale = float(rows * n_seq * n_dp) ** (-0.5)
-    gr, gw = bring_back(at, g, dy, scale)
+    gr, gw = rest(make_bias(idx, cnt), x, d, dy, scale)
     dq, dk, dv = pl.pallas_call(
         unpack_kernel, out_shape=(flat,) * 3, grid=(tiles,), in_specs=[pairs],
         out_specs=(wide(rows, cols),) * 3, cost_estimate=cost(0, q, k, v, packed), name="unpack",

time: 274 us -> 243 us (0.89); the launches traced: 269 us -> 241 us
  Pallas kernels: 262 us -> 238 us
  local copies, waits for them, and re-layouts: 5.67 us -> 2.22 us
    pallas_call x2 -> x1, Pallas kernels: 169 us -> 145 us  [rest(): pl.pallas_call(functools.partial(rest_kernel, scale), out_shape=(jax.Shap...]
    unnamed x12 -> x5, local copies, waits for them, and re-layouts: 4.92 us -> 1.38 us
where the time goes in v4:
time: 243 us; the launch traced here: 241 us
  Pallas kernels  238 us (98%)
    pallas_call x1, Pallas kernels, rest(): pl.pallas_call(functools.partial(rest_kernel, scale), out_shape=(jax.Shap...  145 us
    pallas_call x1, Pallas kernels, local(): pl.pallas_call(front_kernel, out_shape=(packed, small), in_specs=[V] * 5,...  88.3 us

profile of v4, /device:TPU:116, one launch (start us, length us, event | category | flops | bytes accessed | tf_op | source)
XLA Modules:
  0.0 241.2 jit_solution(13165812324970958865)
XLA Ops:
  0.6 0.0 copy-start
  0.6 0.7 copy-done
  1.4 0.7 add_select_fusion
  2.1 0.1 fusion.1
  2.2 0.1 copy.13
  2.3 0.7 select_n.22.bias_ref
  3.0 88.3 %front.1 = (bf16[8,1728,128]{2,1,0:T(8,128)(2,1)}, bf16[8,576,128]{2,1,0:T(8,128)(2,1)}) custom-call(bf16[384,1536]{1,0:T(8,128)(2,1)} %bitcast.9, bf16[384,1536]{1,0:T(8,128)(2,1)} %bitcast.10, bf16[384,1536]{1,0:T(8,128)(2,1)} %bitcast.11, bf16[384,3072]{1,0:T(8,128)(2,1)} %bitcast.7, bf16[96,3072]{1,0:T(8,128)(2,1)} %w_ref.1), custom_call_target="tpu_custom_call" | custom-call | flops 3623878656 | bytes 9437184 | tf_op jit(solution)/shard_map/front/pallas_call | solution.py:568
  91.3 144.5 %rest.1 = (bf16[8,1728,128]{2,1,0:T(8,128)(2,1)}, f32[12,3072]{1,0:T(8,128)}) custom-call(f32[648]{0:T(1024)} %select_n.22.bias_ref, bf16[8,1728,128]{2,1,0:T(8,128)(2,1)} %get-tuple-element.11.x_ref, bf16[8,576,128]{2,1,0:T(8,128)(2,1)} %get-tuple-element.12.d_ref, bf16[384,3072]{1,0:T(8,128)(2,1)} %bitcast.8), custom_call_target="tpu_custom_call" | custom-call | flops 3623878656 | bytes 10616832 | tf_op jit(solution)/shard_map/rest/pallas_call | solution.py:507
  235.8 0.0 copy-start.1
  235.8 4.7 %unpack.1 = (bf16[384,1536]{1,0:T(8,128)(2,1)}, bf16[384,1536]{1,0:T(8,128)(2,1)}, bf16[384,1536]{1,0:T(8,128)(2,1)}) custom-call(bf16[8,1728,128]{2,1,0:T(8,128)(2,1)} %get-tuple-element.13.x_ref), custom_call_target="tpu_custom_call" | custom-call | bytes 7077888 | tf_op jit(solution)/shard_map/unpack/pallas_call | solution.py:591
  240.5 0.0 copy-done.1
  240.5 0.7 copy.15
  (3 shorter events, 0.0 us)
Async XLA Ops:
  0.6 0.7 copy-start
  235.8 4.7 %copy-start.1 = (f32[12,3072]{1,0:T(8,128)S(1)}, f32[12,3072]{1,0:T(8,128)}, u32[]{:S(2)}) copy-start(f32[12,3072]{1,0:T(8,128)} %get-tuple-element.25) | copy-start | bytes 442372

commit v5 on v4

--- a/solution.py
+++ b/solution.py
@@ -284,8 +284,9 @@
     dp, me = lax.axis_index("dp"), lax.axis_index("seq")
     core, zz, lo = dp % 2, (dp // 2) % 4, dp // 8
     sib = dp + 1 - 2 * core
-    tiles, nz, slabs, srows, tcols = part.shape
+    rounds, ways, nz, four, srows, tcols = part.shape
     peers = at_ref.shape[0]
+    slabs = plane.shape[0]
     feats = at_ref.shape[1] // TB
     tb = TB
     cols = dyx.shape[2]
@@ -343,9 +344,71 @@
     def forward(s, k):
         return remote(atr.at[0, s], atr.at[1, s], fw_s.at[k], fw_r.at[k], {"dp": sib})
 
-    def arrived(k):
-        at_copy(k).wait_recv()
-        forward(lax.rem(me - k + peers, peers), k).start()
+    def group(r, g):
+        return lax.rem(me - 2 * r - 1 - g + 2 * peers, peers)
+
+    def place(r, g):
+        return lax.rem(2 * r + 1 + g, peers)
+
+    def arrived(r, both=True):
+        for g in range(2 if both else 1):
+            at_copy(place(r, g)).wait_recv()
+            forward(group(r, g), place(r, g)).start()
+
+    def hop(r, w, step):
+        up = 1 - 2 * w
+        chunk = lax.rem(zz - up * (1 + step) + 2 * nz, nz)
+        return remote(
+            part.at[r, w, chunk], ring.at[r, w, step], z_s.at[r, w, step], z_r.at[r, w, step], {"dp": at_z(up)}
+        )
+
+    def products(r):
+        for g in range(2):
+            forward(group(r, g), place(r, g)).wait_recv()
+        lhs = jnp.concatenate(
+            [
+                jnp.concatenate(
+                    [atr[q, group(r, g), b * feats : (b + 1) * feats, :] for q in range(2) for b in range(tb)],
+                    axis=1,
+                )
+                for g in range(2)
+            ],
+            axis=0,
+        )
+        wide_tile = 2 * BLK
+        for w in range(ways):
+            for c in range(tcols // wide_tile):
+                tc = slice(c * wide_tile, (c + 1) * wide_tile)
+                rc = slice(w * tcols + c * wide_tile, w * tcols + (c + 1) * wide_tile)
+                rhs = jnp.concatenate([dyx[q, :, rc] for q in range(2)], axis=0)
+                prod = lax.dot_general(lhs, rhs, NN, preferred_element_type=F32)
+                for a in range(four):
+                    for z in range(nz):
+                        at = (a * nz + z) * srows
+                        part[r, w, z, a, :, tc] = prod[at : at + srows].astype(BF16)
+            hop(r, w, 0).start()
+
+    def add(r, step):
+        for w in range(ways):
+            hop(r, w, step).wait_recv()
+            chunk = lax.rem(zz - (1 - 2 * w) * (2 + step) + 2 * nz, nz)
+            part[r, w, chunk] = (part[r, w, chunk].astype(F32) + ring[r, w, step].astype(F32)).astype(BF16)
+            if step < nz - 2:
+                hop(r, w, step + 1).start()
+
+    def slab(r, a):
+        where = {"dp": (a % 2) * 8 + zz * 2 + core, "seq": group(r, a // 2)}
+        return remote(part.at[r, :, zz, a], plane.at[my], p_s.at[r, a], p_r.at[my], where)
+
+    def other_slab(r, a, f):
+        @pl.when((group(r, a // 2) != me) | (lo != a % 2))
+        def _():
+            f(slab(r, a))
+
+    def spread(r):
+        add(r, nz - 2)
+        for a in range(four):
+            other_slab(r, a, lambda c: c.start())
 
     def key_rows(h, t):
         return pl.ds(pl.multiple_of((h * tb + t) * BLK, BLK), BLK)
@@ -365,7 +428,10 @@
             for t in range(tb):
                 g_ref[c, key_rows(h, t), :] = acc[h, seq_rows(c * tb + t), :].astype(BF16)
 
-    @pl.loop(0, peers // 2)
+    dy_copy.wait_recv()
+    own_dy.wait()
+
+    @pl.loop(0, rounds)
     def _(pair):
         @pl.loop(0, tb)
         def _(u):
@@ -375,20 +441,35 @@
                 bias_ref, x_ref, d_ref, kvt, acc, at_ref, g_ref,
             )
 
+            @pl.when((u == 0) & (pair > 1))
+            def _():
+                add(pair - 2, 0)
+
+            @pl.when((u == 1) & (pair > 0))
+            def _():
+                arrived(pair - 1)
+
+            @pl.when((u == 1) & (pair > 1))
+            def _():
+                add(pair - 2, 1)
+
         at_copy(2 * pair + 1).start()
         q_copy(2 * pair + 1).start()
 
-        @pl.when(pair < peers // 2 - 1)
+        @pl.when(pair < rounds - 1)
         def _():
             at_copy(2 * pair + 2).start()
             q_copy(2 * pair + 2).start()
 
         @pl.when(pair > 0)
         def _():
-            arrived(2 * pair - 1)
-            arrived(2 * pair)
-
-        @pl.when(pair == peers // 2 - 2)
+            products(pair - 1)
+
+        @pl.when(pair > 1)
+        def _():
+            spread(pair - 2)
+
+        @pl.when(pair == rounds - 2)
         def _():
             for k in (3, 4):
                 settle(k)
@@ -396,74 +477,34 @@
 
     own_at = pltpu.make_async_copy(at_ref.at[me], atr.at[0, me], loc.at[1])
     own_at.start()
+    last = rounds - 1
     late = (1, 2, *range(5, peers))
-    for k in (*late, 0):
-        settle(k)
+    settle(1)
+    settle(2)
+    own_at.wait()
+    forward(me, 0).start()
+    add(last - 1, 0)
+    arrived(last, False)
+    for k in late:
+        if k > 2:
+            settle(k)
+        g_copy(k).start()
+    settle(0)
     own_g = pltpu.make_async_copy(g_ref.at[me], gr_ref.at[me], loc.at[2])
     own_g.start()
-    own_at.wait()
-    forward(me, 0).start()
-    arrived(peers - 1)
-    for k in late:
-        g_copy(k).start()
-
-    @pl.loop(0, peers)
-    def _(k):
-        forward(lax.rem(me - k + peers, peers), k).wait_recv()
-
-    dy_copy.wait_recv()
-    own_dy.wait()
-
-    way = tiles // 2
-
-    def z_copy(t, step):
-        up = 1 if t < way else -1
-        chunk = lax.rem(zz - up * (1 + step) + 2 * nz, nz)
-        return chunk, remote(
-            part.at[t, chunk], ring.at[t, step], z_s.at[t, step], z_r.at[t, step], {"dp": at_z(up)}
-        )
-
-    order = [t + w for t in range(way) for w in (0, way)]
-    for t in order:
-        tc = slice(t * tcols, (t + 1) * tcols)
-
-        @pl.loop(0, peers)
-        def _(s):
-            lhs = jnp.concatenate(
-                [atr[q, s, b * feats : (b + 1) * feats, :] for q in range(2) for b in range(tb)], axis=1
-            )
-            rhs = jnp.concatenate([dyx[q, :, tc] for q in range(2)], axis=0)
-            prod = lax.dot_general(lhs, rhs, NN, preferred_element_type=F32)
-            for j in range(2):
-                for z in range(nz):
-                    r = (j * nz + z) * srows
-                    part[t, z, s * 2 + j] = prod[r : r + srows].astype(BF16)
-
-        z_copy(t, 0)[1].start()
-
-    for step in range(nz - 1):
-        for t in order:
-            z_copy(t, step)[1].wait_recv()
-            up = 1 if t < way else -1
-            chunk = lax.rem(zz - up * (2 + step) + 2 * nz, nz)
-            part[t, chunk] = (part[t, chunk].astype(F32) + ring[t, step].astype(F32)).astype(BF16)
-            if step < nz - 2:
-                z_copy(t, step + 1)[1].start()
-
-    def p_copy(k):
-        j, where = plane_peer(k)
-        return remote(part.at[:, zz, j], plane.at[k], p_s.at[k], p_r.at[k], where)
+    products(last)
+    add(last - 1, 1)
+    add(last, 0)
+    spread(last - 1)
+    add(last, 1)
+    spread(last)
+    total[...] = part[last, :, zz, 2 + lo].astype(F32)
 
     @pl.loop(1, slabs)
     def _(k):
-        p_copy(k).start()
-
-    total[...] = part[:, zz, my].astype(F32)
-
-    @pl.loop(1, slabs)
-    def _(k):
-        p_copy(k).wait_recv()
-        total[...] += plane[k].astype(F32)
+        j, where = plane_peer(k)
+        remote(plane.at[j], plane.at[j], p_s.at[0, 0], p_r.at[j], where).wait_recv()
+        total[...] += plane[j].astype(F32)
 
     rows = gw_ref.shape[0]
     for c in range(2):
@@ -471,7 +512,7 @@
     swap = remote(half.at[1 - core], other, o_s, o_r, {"dp": sib})
     swap.start()
     swap.wait_recv()
-    for t in range(tiles):
+    for t in range(ways):
         gw_ref[:, pl.ds(pl.multiple_of(core * cols + t * tcols, BLK), tcols)] = half[core, t]
         gw_ref[:, pl.ds(pl.multiple_of((1 - core) * cols + t * tcols, BLK), tcols)] = other[t]
 
@@ -487,19 +528,20 @@
         q_copy(k).wait()
         g_copy(k).wait()
 
-    for step in range(nz - 1):
-        for t in order:
-            z_copy(t, step)[1].wait_send()
-
-    @pl.loop(1, slabs)
-    def _(k):
-        p_copy(k).wait_send()
+    @pl.loop(0, rounds)
+    def _(r):
+        for w in range(ways):
+            for step in range(nz - 1):
+                hop(r, w, step).wait_send()
+        for a in range(four):
+            other_slab(r, a, lambda c: c.wait_send())
 
 
 def rest(bias, x, d, dy, scale):
     peers = x.shape[0]
     rows, depth = dy.shape
-    tiles, tcols, nz, slabs = 6, 256, 4, 16
+    rounds, ways, nz, slabs = 4, 2, 4, 16
+    tcols = depth // 2 // ways
     feats = d.shape[1] // TB
     heads, seq = feats // HDIM, peers * TB * BLK
     out_rows = peers * feats // 128
@@ -516,16 +558,16 @@
             pltpu.VMEM((heads, seq, BLK), F32),
             pltpu.VMEM((2, *d.shape), BF16),
             pltpu.VMEM((2, rows, depth // 2), BF16),
-            pltpu.VMEM((tiles, nz, slabs, 2 * out_rows, tcols), BF16),
-            pltpu.VMEM((tiles, nz - 1, slabs, 2 * out_rows, tcols), BF16),
-            pltpu.VMEM((slabs, tiles, 2 * out_rows, tcols), BF16),
-            pltpu.VMEM((tiles, 2 * out_rows, tcols), F32),
-            pltpu.VMEM((2, tiles, out_rows, tcols), F32),
-            pltpu.VMEM((tiles, out_rows, tcols), F32),
+            pltpu.VMEM((rounds, ways, nz, 4, 2 * out_rows, tcols), BF16),
+            pltpu.VMEM((rounds, ways, nz - 1, 4, 2 * out_rows, tcols), BF16),
+            pltpu.VMEM((slabs, ways, 2 * out_rows, tcols), BF16),
+            pltpu.VMEM((ways, 2 * out_rows, tcols), F32),
+            pltpu.VMEM((2, ways, out_rows, tcols), F32),
+            pltpu.VMEM((ways, out_rows, tcols), F32),
             dma((peers,)), dma((peers,)), dma((peers,)), dma((peers,)), dma, dma,
             dma((peers,)), dma((peers,)), dma((peers,)), dma((peers,)),
-            dma((tiles, nz - 1)), dma((tiles, nz - 1)),
-            dma((slabs,)), dma((slabs,)), dma, dma, dma((3,)),
+            dma((rounds, ways, nz - 1)), dma((rounds, ways, nz - 1)),
+            dma((rounds, 4)), dma((slabs,)), dma, dma, dma((3,)),
         ],
         compiler_params=pltpu.CompilerParams(
             collective_id=1, has_side_effects=True, vmem_limit_bytes=60 * 2**20

time: 243 us -> 227 us (0.934)
  the two profiles are of different devices: /device:TPU:116 before, /device:TPU:47 now
where the time goes in v5:
time: 227 us
  Pallas kernels  223 us (98%)
    pallas_call x1, Pallas kernels, rest(): pl.pallas_call(functools.partial(rest_kernel, scale), out_shape=(jax.Shap...  139 us
    pallas_call x1, Pallas kernels, local(): pl.pallas_call(front_kernel, out_shape=(packed, small), in_specs=[V] * 5,...  79.8 us
    pallas_call x1, Pallas kernels, local(): pl.pallas_call(unpack_kernel, out_shape=(flat,) * 3, grid=(tiles,), in_sp...  4.72 us

profile of v5, /device:TPU:47, one launch (start us, length us, event | category | flops | bytes accessed | tf_op | source)
XLA Modules:
  0.0 226.8 jit_solution(7700398098594316773)
XLA Ops:
  0.6 0.0 copy-start
  0.6 0.7 copy-done
  1.4 0.7 add_select_fusion
  2.1 0.1 fusion.1
  2.2 0.1 copy.13
  2.3 0.7 select_n.22.bias_ref
  3.0 79.8 %front.1 = (bf16[8,1728,128]{2,1,0:T(8,128)(2,1)}, bf16[8,576,128]{2,1,0:T(8,128)(2,1)}) custom-call(bf16[384,1536]{1,0:T(8,128)(2,1)} %bitcast.9, bf16[384,1536]{1,0:T(8,128)(2,1)} %bitcast.10, bf16[384,1536]{1,0:T(8,128)(2,1)} %bitcast.11, bf16[384,3072]{1,0:T(8,128)(2,1)} %bitcast.7, bf16[96,3072]{1,0:T(8,128)(2,1)} %w_ref.1), custom_call_target="tpu_custom_call" | custom-call | flops 3623878656 | bytes 9437184 | tf_op jit(solution)/shard_map/front/pallas_call | solution.py:610
  82.8 138.6 %rest.1 = (bf16[8,1728,128]{2,1,0:T(8,128)(2,1)}, f32[12,3072]{1,0:T(8,128)}) custom-call(f32[648]{0:T(1024)} %select_n.22.bias_ref, bf16[8,1728,128]{2,1,0:T(8,128)(2,1)} %get-tuple-element.11.x_ref, bf16[8,576,128]{2,1,0:T(8,128)(2,1)} %get-tuple-element.12.d_ref, bf16[384,3072]{1,0:T(8,128)(2,1)} %bitcast.8), custom_call_target="tpu_custom_call" | custom-call | flops 3623878656 | bytes 10616832 | tf_op jit(solution)/shard_map/rest/pallas_call | solution.py:549
  221.4 0.0 copy-start.1
  221.4 4.7 %unpack.1 = (bf16[384,1536]{1,0:T(8,128)(2,1)}, bf16[384,1536]{1,0:T(8,128)(2,1)}, bf16[384,1536]{1,0:T(8,128)(2,1)}) custom-call(bf16[8,1728,128]{2,1,0:T(8,128)(2,1)} %get-tuple-element.13.x_ref), custom_call_target="tpu_custom_call" | custom-call | bytes 7077888 | tf_op jit(solution)/shard_map/unpack/pallas_call | solution.py:633
  226.1 0.0 copy-done.1
  226.1 0.7 copy.15
  (3 shorter events, 0.0 us)
Async XLA Ops:
  0.6 0.7 copy-start
  221.4 4.7 %copy-start.1 = (f32[12,3072]{1,0:T(8,128)S(1)}, f32[12,3072]{1,0:T(8,128)}, u32[]{:S(2)}) copy-start(f32[12,3072]{1,0:T(8,128)} %get-tuple-element.25) | copy-start | bytes 442372

commit v6 on v5

--- a/solution.py
+++ b/solution.py
@@ -20,8 +20,8 @@
 Q_AT = 1152
 
 
-def front_kernel(q_ref, k_ref, v_ref, dy_ref, w_ref, xr_ref, dr_ref, xs, ds, wall,
-                 x_s, x_r, d_s, d_r, z_s, z_r, y_s, y_r, f_s, f_r, loc):
+def bring_in(meanwhile, q_ref, k_ref, v_ref, dy_ref, w_ref, xr_ref, dr_ref, xs, ds, wall,
+             x_s, x_r, d_s, d_r, z_s, z_r, y_s, y_r, f_s, f_r, loc):
     dp, me = lax.axis_index("dp"), lax.axis_index("seq")
     core, zz, lo = dp % 2, (dp // 2) % 4, dp // 8
     sib, mate = dp + 1 - 2 * core, dp + 8 - 16 * lo
@@ -32,19 +32,6 @@
 
     def at_z(k):
         return lo * 8 + lax.rem(zz + k + nz, nz) * 2 + core
-
-    bar = pltpu.get_barrier_semaphore()
-
-    def hello(where):
-        pl.semaphore_signal(bar, inc=1, device_id=where, device_id_type=MESH)
-
-    @pl.loop(1, peers)
-    def _(k):
-        hello({"seq": lax.rem(me + k, peers)})
-
-    for where in (sib, mate, at_z(1), at_z(-1)):
-        hello({"dp": where})
-    pl.semaphore_wait(bar, peers + 3)
 
     def remote(src, dst, ssem, rsem, where):
         return pltpu.make_async_remote_copy(
@@ -191,6 +178,7 @@
     def _(k):
         x_copy(k).wait()
 
+    meanwhile()
     for n, (l, k) in enumerate(order):
         s = peer(l, k)
 
@@ -279,8 +267,9 @@
     return jnp.where(hit, 0.0, -1e30).astype(F32).reshape(-1)
 
 
-def rest_kernel(scale, bias_ref, x_ref, d_ref, dy_ref, gr_ref, gw_ref, at_ref, g_ref, kvt, acc, atr, dyx, part, ring, plane, total, half, other,
-                at_s, at_r, fw_s, fw_r, dy_s, dy_r, q_s, q_r, g_s, g_r, z_s, z_r, p_s, p_r, o_s, o_r, loc):
+def whole_kernel(scale, bias_ref, q_ref, k_ref, v_ref, dy_ref, w_ref, gr_ref, gw_ref,
+                 x_ref, d_ref, wall, at_ref, g_ref, kvt, acc, atr, dyx, part, ring, plane, total, half, other,
+                at_s, at_r, fw_s, fw_r, dy_s, dy_r, q_s, q_r, g_s, g_r, z_s, z_r, p_s, p_r, o_s, o_r, loc, *in_sems):
     dp, me = lax.axis_index("dp"), lax.axis_index("seq")
     core, zz, lo = dp % 2, (dp // 2) % 4, dp // 8
     sib = dp + 1 - 2 * core
@@ -318,6 +307,23 @@
             src_ref=src, dst_ref=dst, send_sem=ssem, recv_sem=rsem, device_id=where, device_id_type=MESH
         )
 
+    heads = acc.shape[0]
+
+    def key_rows(h, t):
+        return pl.ds(pl.multiple_of((h * tb + t) * BLK, BLK), BLK)
+
+    def seq_rows(b):
+        return pl.ds(pl.multiple_of(b * BLK, BLK), BLK)
+
+    def turn():
+        @pl.loop(0, peers * tb)
+        def _(j):
+            for h in range(heads):
+                kvt[h, :, seq_rows(j)] = x_ref[j // tb, key_rows(h, lax.rem(j, tb)), :].T
+                acc[h, seq_rows(j), :] = jnp.zeros((BLK, BLK), F32)
+
+    bring_in(turn, q_ref, k_ref, v_ref, dy_ref, w_ref, x_ref, d_ref, g_ref, at_ref, wall, *in_sems)
+
     def at_copy(k):
         p = lax.rem(me + k, peers)
         return remote(at_ref.at[p], atr.at[0, me], at_s.at[k], at_r.at[k], {"seq": p})
@@ -328,8 +334,6 @@
     dy_copy.start()
     own_dy = pltpu.make_async_copy(dy_ref.at[:, mine], dyx.at[0], loc.at[0])
     own_dy.start()
-
-    heads = acc.shape[0]
 
     def q_copy(k):
         p = lax.rem(me + k, peers)
@@ -410,18 +414,6 @@
         for a in range(four):
             other_slab(r, a, lambda c: c.start())
 
-    def key_rows(h, t):
-        return pl.ds(pl.multiple_of((h * tb + t) * BLK, BLK), BLK)
-
-    def seq_rows(b):
-        return pl.ds(pl.multiple_of(b * BLK, BLK), BLK)
-
-    @pl.loop(0, peers * tb)
-    def _(j):
-        for h in range(heads):
-            kvt[h, :, seq_rows(j)] = x_ref[j // tb, key_rows(h, lax.rem(j, tb)), :].T
-            acc[h, seq_rows(j), :] = jnp.zeros((BLK, BLK), F32)
-
     def settle(k):
         c = lax.rem(me + k, peers)
         for h in range(heads):
@@ -537,21 +529,26 @@
             other_slab(r, a, lambda c: c.wait_send())
 
 
-def rest(bias, x, d, dy, scale):
-    peers = x.shape[0]
+def whole(bias, q, k, v, dy, w, peers, scale):
     rows, depth = dy.shape
+    hd = q.shape[1]
     rounds, ways, nz, slabs = 4, 2, 4, 16
     tcols = depth // 2 // ways
-    feats = d.shape[1] // TB
+    feats = hd // peers
+    x = jax.ShapeDtypeStruct((peers, feats // HDIM * rows + TB * feats, BLK), BF16)
+    d = jax.ShapeDtypeStruct((peers, TB * feats, BLK), BF16)
     heads, seq = feats // HDIM, peers * TB * BLK
     out_rows = peers * feats // 128
     dma = pltpu.SemaphoreType.DMA
     return pl.pallas_call(
-        functools.partial(rest_kernel, scale),
+        functools.partial(whole_kernel, scale),
         out_shape=(jax.ShapeDtypeStruct(x.shape, BF16), jax.ShapeDtypeStruct((out_rows, depth), F32)),
-        in_specs=[S, V, V, V],
+        in_specs=[S, V, V, V, V, V],
         out_specs=(V, V),
         scratch_shapes=[
+            pltpu.VMEM(x.shape, BF16),
+            pltpu.VMEM(d.shape, BF16),
+            pltpu.VMEM((2, 2, nz, *w.shape), BF16),
             pltpu.VMEM(d.shape, BF16),
             pltpu.VMEM(x.shape, BF16),
             pltpu.VMEM((heads, BLK, seq), BF16),
@@ -568,13 +565,15 @@
             dma((peers,)), dma((peers,)), dma((peers,)), dma((peers,)),
             dma((rounds, ways, nz - 1)), dma((rounds, ways, nz - 1)),
             dma((rounds, 4)), dma((slabs,)), dma, dma, dma((3,)),
+            dma((peers,)), dma((peers,)), dma((peers,)), dma((peers,)),
+            dma((2, 2, 2)), dma((2, 2, 2)), dma, dma, dma((2, 4)), dma((2, 4)), dma((3,)),
         ],
         compiler_params=pltpu.CompilerParams(
-            collective_id=1, has_side_effects=True, vmem_limit_bytes=60 * 2**20
+            collective_id=0, has_side_effects=True, vmem_limit_bytes=60 * 2**20
         ),
-        cost_estimate=cost(2 * rows * depth * peers * feats, x, d, x, dy),
-        name="rest",
-    )(bias, x, d, dy)
+        cost_estimate=cost(4 * rows * depth * hd, q, k, v, dy, x),
+        name="whole",
+    )(bias, q, k, v, dy, w)
 
 
 V = pl.BlockSpec(memory_space=pltpu.VMEM)
@@ -593,43 +592,21 @@
 
 def local(query, key_states, value_states, grad_out, w_out, block_index, block_count):
     rows, hd = query.shape[1:]
-    depth = grad_out.shape[2]
     n_seq, n_dp = lax.axis_size("seq"), lax.axis_size("dp")
     per = hd // HDIM // n_seq
     tiles = n_seq // 2
     cols = hd // tiles
     x_rows = per * rows + TB * per * HDIM
-    d_rows = TB * per * HDIM
     packed = jax.ShapeDtypeStruct((n_seq, x_rows, BLK), BF16)
-    small = jax.ShapeDtypeStruct((n_seq, d_rows, BLK), BF16)
     pairs = pl.BlockSpec((2, x_rows, BLK), lambda t: (t, 0, 0))
     flat = jax.ShapeDtypeStruct((rows, hd), BF16)
     q, k, v, dy = query[0], key_states[0], value_states[0], grad_out[0]
 
-    dma = pltpu.SemaphoreType.DMA
-    x, d = pl.pallas_call(
-        front_kernel,
-        out_shape=(packed, small),
-        in_specs=[V] * 5,
-        out_specs=(V, V),
-        scratch_shapes=[
-            pltpu.VMEM(packed.shape, BF16),
-            pltpu.VMEM(small.shape, BF16),
-            pltpu.VMEM((2, 2, n_dp // 4, *w_out.shape), BF16),
-            dma((n_seq,)), dma((n_seq,)), dma((n_seq,)), dma((n_seq,)),
-            dma((2, 2, 2)), dma((2, 2, 2)), dma, dma, dma((2, 4)), dma((2, 4)), dma((3,)),
-        ],
-        compiler_params=pltpu.CompilerParams(
-            collective_id=0, has_side_effects=True, vmem_limit_bytes=56 * 2**20
-        ),
-        cost_estimate=cost(2 * rows * depth * hd, q, k, v, dy, packed),
-        name="front",
-    )(q, k, v, dy, w_out)
     first = lax.axis_index("seq") * per
     idx = lax.dynamic_slice_in_dim(block_index, first, per, 0)
     cnt = lax.dynamic_slice_in_dim(block_count, first, per, 0)
     scale = float(rows * n_seq * n_dp) ** (-0.5)
-    gr, gw = rest(make_bias(idx, cnt), x, d, dy, scale)
+    gr, gw = whole(make_bias(idx, cnt), q, k, v, dy, w_out, n_seq, scale)
     dq, dk, dv = pl.pallas_call(
         unpack_kernel, out_shape=(flat,) * 3, grid=(tiles,), in_specs=[pairs],
         out_specs=(wide(rows, cols),) * 3, cost_estimate=cost(0, q, k, v, packed), name="unpack",

time: 227 us -> 228 us (level)
  the two profiles are of different devices: /device:TPU:47 before, /device:TPU:15 now
where the time goes in v6:
time: 228 us; the launch traced here: 227 us
  Pallas kernels  224 us (98%)
    pallas_call x1, Pallas kernels, whole(): pl.pallas_call(functools.partial(whole_kernel, scale), out_shape=(jax.Sha...  219 us
    pallas_call x1, Pallas kernels, local(): pl.pallas_call(unpack_kernel, out_shape=(flat,) * 3, grid=(tiles,), in_sp...  4.72 us

profile of v6, /device:TPU:15, one launch (start us, length us, event | category | flops | bytes accessed | tf_op | source)
XLA Modules:
  0.0 227.2 jit_solution(3726077677960803007)
XLA Ops:
  0.6 0.0 copy-start
  0.6 0.7 copy-done
  1.4 0.7 add_select_fusion
  2.1 0.1 fusion.1
  2.2 0.1 copy.13
  2.3 0.7 select_n.22.bias_ref
  3.0 218.8 %whole.1 = (bf16[8,1728,128]{2,1,0:T(8,128)(2,1)}, f32[12,3072]{1,0:T(8,128)}) custom-call(f32[648]{0:T(1024)} %select_n.22.bias_ref, bf16[384,1536]{1,0:T(8,128)(2,1)} %bitcast.8, bf16[384,1536]{1,0:T(8,128)(2,1)} %bitcast.9, bf16[384,1536]{1,0:T(8,128)(2,1)} %bitcast.10, bf16[384,3072]{1,0:T(8,128)(2,1)} %bitcast.7, bf16[96,3072]{1,0:T(8,128)(2,1)} %w_ref.1), custom_call_target="tpu_custom_call" | custom-call | flops 7247757312 | bytes 9437184 | tf_op jit(solution)/shard_map/whole/pallas_call | solution.py:543
  221.8 0.0 copy-start.1
  221.8 4.7 %unpack.1 = (bf16[384,1536]{1,0:T(8,128)(2,1)}, bf16[384,1536]{1,0:T(8,128)(2,1)}, bf16[384,1536]{1,0:T(8,128)(2,1)}) custom-call(bf16[8,1728,128]{2,1,0:T(8,128)(2,1)} %get-tuple-element.9.x_ref), custom_call_target="tpu_custom_call" | custom-call | bytes 7077888 | tf_op jit(solution)/shard_map/unpack/pallas_call | solution.py:610
  226.5 0.0 copy-done.1
  226.5 0.7 copy.15
  (3 shorter events, 0.0 us)
Async XLA Ops:
  0.6 0.7 copy-start
  221.8 4.7 %copy-start.1 = (f32[12,3072]{1,0:T(8,128)S(1)}, f32[12,3072]{1,0:T(8,128)}, u32[]{:S(2)}) copy-start(f32[12,3072]{1,0:T(8,128)} %get-tuple-element.21) | copy-start | bytes 442372

commit v7 on v5

--- a/solution.py
+++ b/solution.py
@@ -431,71 +431,61 @@
     dy_copy.wait_recv()
     own_dy.wait()
 
-    @pl.loop(0, rounds)
-    def _(pair):
-        @pl.loop(0, tb)
-        def _(u):
-            b0 = (me + 1 + 2 * pair) * tb + 2 * u
-            attend(
-                [(h, lax.rem(b0 + t, peers * tb)) for t in range(2) for h in range(heads)],
-                bias_ref, x_ref, d_ref, kvt, acc, at_ref, g_ref,
-            )
-
-            @pl.when((u == 0) & (pair > 1))
-            def _():
-                add(pair - 2, 0)
-
-            @pl.when((u == 1) & (pair > 0))
-            def _():
-                arrived(pair - 1)
-
-            @pl.when((u == 1) & (pair > 1))
-            def _():
-                add(pair - 2, 1)
-
-        at_copy(2 * pair + 1).start()
-        q_copy(2 * pair + 1).start()
-
-        @pl.when(pair < rounds - 1)
-        def _():
-            at_copy(2 * pair + 2).start()
-            q_copy(2 * pair + 2).start()
-
-        @pl.when(pair > 0)
-        def _():
-            products(pair - 1)
-
-        @pl.when(pair > 1)
-        def _():
-            spread(pair - 2)
-
-        @pl.when(pair == rounds - 2)
-        def _():
-            for k in (3, 4):
-                settle(k)
-                g_copy(k).start()
+    @pl.loop(0, peers)
+    def _(n):
+        b0 = (me + 1 + n) * tb
+        attend(
+            [(h, lax.rem(b0 + t, peers * tb)) for t in range(tb) for h in range(heads)],
+            bias_ref, x_ref, d_ref, kvt, acc, at_ref, g_ref,
+        )
+        even = n % 2 == 0
+
+        @pl.when(n < peers - 1)
+        def _():
+            at_copy(n + 1).start()
+
+        @pl.when(even & (n > 3))
+        def _():
+            add((n - 4) // 2, 1)
+
+        @pl.when((n % 2 == 1) & (n > 2))
+        def _():
+            add((n - 3) // 2, 0)
+
+        @pl.when(even & (n > 1))
+        def _():
+            arrived((n - 2) // 2)
+            products((n - 2) // 2)
+
+        @pl.when((n % 2 == 1) & (n > 4))
+        def _():
+            spread((n - 5) // 2)
+
+        @pl.when(n < peers - 1)
+        def _():
+            q_copy(n + 1).start()
+
+        @pl.when((n > 3) & (n < peers - 1))
+        def _():
+            settle(n - 1)
+            g_copy(n - 1).start()
 
     own_at = pltpu.make_async_copy(at_ref.at[me], atr.at[0, me], loc.at[1])
     own_at.start()
     last = rounds - 1
-    late = (1, 2, *range(5, peers))
-    settle(1)
-    settle(2)
+    arrived(last, False)
     own_at.wait()
     forward(me, 0).start()
-    add(last - 1, 0)
-    arrived(last, False)
-    for k in late:
-        if k > 2:
-            settle(k)
+    add(last - 1, 1)
+    products(last)
+    for k in (1, 2, peers - 2, peers - 1):
+        settle(k)
         g_copy(k).start()
+    spread(last - 1)
     settle(0)
     own_g = pltpu.make_async_copy(g_ref.at[me], gr_ref.at[me], loc.at[2])
     own_g.start()
-    products(last)
-    add(last - 1, 1)
     add(last, 0)
-    spread(last - 1)
     add(last, 1)
     spread(last)
     total[...] = part[last, :, zz, 2 + lo].astype(F32)

time: 227 us -> 219 us (0.965)
  the two profiles are of different devices: /device:TPU:47 before, /device:TPU:116 now
where the time goes in v7:
time: 219 us; the launch traced here: 218 us
  Pallas kernels  215 us (98%)
  local copies, waits for them, and re-layouts  2.22 us (1%)
    pallas_call x1, Pallas kernels, rest(): pl.pallas_call(functools.partial(rest_kernel, scale), out_shape=(jax.Shap...  122 us
    pallas_call x1, Pallas kernels, local(): pl.pallas_call(front_kernel, out_shape=(packed, small), in_specs=[V] * 5,...  88.3 us
    pallas_call x1, Pallas kernels, local(): pl.pallas_call(unpack_kernel, out_shape=(flat,) * 3, grid=(tiles,), in_sp...  4.72 us

profile of v7, /device:TPU:116, one launch (start us, length us, event | category | flops | bytes accessed | tf_op | source)
XLA Modules:
  0.0 218.3 jit_solution(13834181082841572568)
XLA Ops:
  0.6 0.0 copy-start
  0.6 0.7 copy-done
  1.4 0.7 add_select_fusion
  2.1 0.1 fusion.1
  2.2 0.1 copy.13
  2.3 0.7 select_n.22.bias_ref
  3.0 88.3 %front.1 = (bf16[8,1728,128]{2,1,0:T(8,128)(2,1)}, bf16[8,576,128]{2,1,0:T(8,128)(2,1)}) custom-call(bf16[384,1536]{1,0:T(8,128)(2,1)} %bitcast.9, bf16[384,1536]{1,0:T(8,128)(2,1)} %bitcast.10, bf16[384,1536]{1,0:T(8,128)(2,1)} %bitcast.11, bf16[384,3072]{1,0:T(8,128)(2,1)} %bitcast.7, bf16[96,3072]{1,0:T(8,128)(2,1)} %w_ref.1), custom_call_target="tpu_custom_call" | custom-call | flops 3623878656 | bytes 9437184 | tf_op jit(solution)/shard_map/front/pallas_call | solution.py:600
  91.3 121.6 %rest.1 = (bf16[8,1728,128]{2,1,0:T(8,128)(2,1)}, f32[12,3072]{1,0:T(8,128)}) custom-call(f32[648]{0:T(1024)} %select_n.22.bias_ref, bf16[8,1728,128]{2,1,0:T(8,128)(2,1)} %get-tuple-element.11.x_ref, bf16[8,576,128]{2,1,0:T(8,128)(2,1)} %get-tuple-element.12.d_ref, bf16[384,3072]{1,0:T(8,128)(2,1)} %bitcast.8), custom_call_target="tpu_custom_call" | custom-call | flops 3623878656 | bytes 10616832 | tf_op jit(solution)/shard_map/rest/pallas_call | solution.py:539
  212.9 0.0 copy-start.1
  212.9 4.7 %unpack.1 = (bf16[384,1536]{1,0:T(8,128)(2,1)}, bf16[384,1536]{1,0:T(8,128)(2,1)}, bf16[384,1536]{1,0:T(8,128)(2,1)}) custom-call(bf16[8,1728,128]{2,1,0:T(8,128)(2,1)} %get-tuple-element.13.x_ref), custom_call_target="tpu_custom_call" | custom-call | bytes 7077888 | tf_op jit(solution)/shard_map/unpack/pallas_call | solution.py:623
  217.6 0.0 copy-done.1
  217.6 0.7 copy.15
  (3 shorter events, 0.0 us)
Async XLA Ops:
  0.6 0.7 copy-start
  212.9 4.7 %copy-start.1 = (f32[12,3072]{1,0:T(8,128)S(1)}, f32[12,3072]{1,0:T(8,128)}, u32[]{:S(2)}) copy-start(f32[12,3072]{1,0:T(8,128)} %get-tuple-element.25) | copy-start | bytes 442372
